TPU v7x, 128 devices: a whole 4x4x4 slice. The times are simulated.
128 devices in a mesh: pix: 8 (over z, core), date: 16 (over y, x).
Axes of the slice: x: 4, y: 4, z: 4, core: 2. Of those that a mesh axis runs over, the one named last changes fastest.
Arguments:
- acquisitions: float32 [2, 288, 32, 1024], P(None, 'date', None, 'pix')
- offsets: int32 [288, 3], P('date'), may hold values from 1 to 4, as said below
Outputs:
- coherence: float32 [288, 3, 32, 1024], P(None, None, 'date', 'pix')
- displacement: float32 [288, 32, 1024], P(None, 'date', 'pix')
Inputs may be any that keep to these rules, and one draw needn't show every extreme that they name: Each row holds 3 distinct offsets, one of them always 4.
All inputs are finite; a program needn't handle non-finite values.
Results may differ from a plain program's by a relative error of at most 0.0001.
Values sent between devices are 32-bit elements; how exact they have to be, the bound alone decides.
No kernel may reach another device: no remote copies, remote signals or barrier semaphores. Data moves between devices by JAX's collectives and lax.ppermute only.
A program may use at most 64 MiB of HBM per device.

v0:
```python
import functools

import jax
import jax.numpy as jnp
from jax import lax
from jax.experimental import pallas as pl
from jax.experimental.pallas import tpu as pltpu
from jax.sharding import PartitionSpec as P

SPAN = 4
K = 3
HR = 2
HC = 7
ITERS = 6
DAMPING = 0.05
EPSILON = 1e-06

LANES = 128
ROWS = 32
GROUPS = ROWS // 8
FIELDS = 80
F32 = jnp.float32
BF16 = jnp.bfloat16


def lanes_of(shape):
    return lax.broadcasted_iota(jnp.int32, shape, len(shape) - 1)


def rows_of(shape):
    return lax.broadcasted_iota(jnp.int32, shape, len(shape) - 2)


def pack_kernel(acq_ref, packed_ref, rim_ref, corner_ref):
    dates = acq_ref.shape[1]
    lane = lanes_of((8, LANES))
    keep = (lane % 16) < 14
    for t in range(dates):
        total = jnp.zeros((8, LANES), F32)
        for f in range(2):
            for g in range(GROUPS):
                begin = 64 * f + 16 * g
                moved = pltpu.roll(acq_ref[f, t, 8 * g : 8 * g + 8, :], begin + HC, 1)
                total = jnp.where((lane >= begin) & (lane < begin + 14), moved, total)
        packed_ref[t] = total
        if t < SPAN:
            corner_ref[t] = total
    rim_ref[...] = acq_ref[:, :SPAN]


def thirds(values):
    high = values.astype(BF16)
    rest = values - high.astype(F32)
    middle = rest.astype(BF16)
    low = (rest - middle.astype(F32)).astype(BF16)
    return jnp.concatenate([high, middle, low], axis=1)


def row_window(parts):
    sub = rows_of((8, LANES))
    zero = jnp.zeros((8, LANES), F32)

    def up(x, n):
        rolled = [pltpu.roll(v, 8 - n, 0) for v in x] + [zero]
        return [jnp.where(sub < 8 - n, rolled[g], rolled[g + 1]) for g in range(GROUPS)]

    def down(x, n, above):
        rolled = [above] + [pltpu.roll(v, n, 0) for v in x]
        return [jnp.where(sub >= n, rolled[g + 1], rolled[g]) for g in range(GROUPS)]

    two = [a + b for a, b in zip(parts, up(parts, 1))]
    above = jnp.where(sub == 1, pltpu.roll(parts[0], 1, 0), 0.0)
    return [a + b + c for a, b, c in zip(parts, up(two, 1), down(two, 2, above))]


def pair_kernel(
    off_ref, acq_ref, rim_ref, left_ref, right_ref, corner_left_ref, corner_right_ref,
    out_ref, ext_ref, halo_ref, turned_ref, power_ref, right_side_ref, *, batch,
):
    dates = acq_ref.shape[1]
    total_dates = dates * lax.axis_size("date")
    first = lax.axis_index("date") * dates
    wide = dates + SPAN

    row = lax.broadcasted_iota(jnp.int32, (LANES, LANES), 0)
    col = lax.broadcasted_iota(jnp.int32, (LANES, LANES), 1)
    band = (jnp.abs(row - col) <= HC).astype(F32).astype(BF16)
    center_band = jnp.concatenate([band] * 3, axis=0)
    place = row % 16
    reach = ((place < HC) & (col <= place)) | (
        (place >= HC) & (place < 2 * HC) & (col >= LANES - 2 * HC + place)
    )
    halo_band = jnp.concatenate(
        [(reach & ((row % 64) // 16 == g)).astype(F32).astype(BF16) for g in range(GROUPS)], axis=1
    )
    halo_band = jnp.concatenate([halo_band] * 3, axis=0)

    ext_ref[:, :dates] = acq_ref[...]
    ext_ref[:, dates:] = rim_ref[...]
    lane = lanes_of((8, LANES))
    from_left = (lane % 16) < HC
    sign = jnp.where(lane < 64, -1.0, 1.0).astype(F32)
    for t in range(wide):
        if t < dates:
            halo = jnp.where(from_left, left_ref[t], right_ref[t])
        else:
            halo = jnp.where(from_left, corner_left_ref[t - dates], corner_right_ref[t - dates])
        halo_ref[t] = halo
        turned_ref[t] = pltpu.roll(halo, 64, 1) * sign
        right_side_ref[t] = jnp.zeros((ROWS, LANES), F32)

    def windows(products, halos):
        n = len(products)
        cols = jnp.dot(
            thirds(jnp.concatenate(products, axis=0)), center_band, preferred_element_type=F32
        )
        rims = jnp.dot(
            thirds(jnp.concatenate(halos, axis=0)), halo_band, preferred_element_type=F32
        )
        return [
            row_window(
                [
                    cols[ROWS * i + 8 * g : ROWS * i + 8 * g + 8]
                    + rims[8 * i : 8 * i + 8, LANES * g : LANES * (g + 1)]
                    for g in range(GROUPS)
                ]
            )
            for i in range(n)
        ]

    per = 11
    def power_step(step, carry):
        products, halos = [], []
        for i in range(per):
            t = step * per + i
            re, im = ext_ref[0, t], ext_ref[1, t]
            products.append(re * re + im * im)
            halos.append(halo_ref[t] * halo_ref[t])
        for i, parts in enumerate(windows(products, halos)):
            t = step * per + i
            for g in range(GROUPS):
                power_ref[t, 8 * g : 8 * g + 8, :] = parts[g]
        return carry

    lax.fori_loop(0, wide // per, power_step, 0)

    def pair_step(step, offsets_row):
        products, halos, seconds = [], [], []
        for i in range(batch):
            t = step * batch + i
            re, im, halo = ext_ref[0, t], ext_ref[1, t], halo_ref[t]
            for k in range(K):
                offset = off_ref[t, k]
                j = t + offset
                seconds.append((t, k, offset, j))
                re2, im2 = ext_ref[0, j], ext_ref[1, j]
                products.append(re * re2 + im * im2)
                products.append(im * re2 - re * im2)
                halos.append(halo * halo_ref[j])
                halos.append(halo * turned_ref[j])
        looked = windows(products, halos)
        for n, (t, k, offset, j) in enumerate(seconds):
            offsets_row = jnp.where(lane == K * t + k, offset.astype(F32), offsets_row)
            usable = jnp.where(first + j < total_dates, 1.0, 0.0).astype(F32)
            for g in range(GROUPS):
                rows = pl.ds(8 * g, 8)
                re, im = looked[2 * n][g], looked[2 * n + 1][g]
                scale = usable * lax.rsqrt(power_ref[t, rows, :] * power_ref[j, rows, :] + EPSILON)
                coherence = jnp.sqrt(re * re + im * im) * scale
                flow = coherence * (im * scale)
                out_ref[pl.ds(4 * g * 2 * FIELDS + K * t + k, 8, stride=FIELDS), :] = coherence
                right_side_ref[t, rows, :] = right_side_ref[t, rows, :] - flow
                right_side_ref[j, rows, :] = right_side_ref[j, rows, :] + flow
        return offsets_row

    offsets_row = lax.fori_loop(0, dates // batch, pair_step, jnp.zeros((8, LANES), F32))
    for g in range(GROUPS):
        base = 4 * g * 2 * FIELDS + K * dates
        for t in range(wide):
            out_ref[pl.ds(base + t, 8, stride=FIELDS), :] = right_side_ref[t, 8 * g : 8 * g + 8, :]
        for f in range(K * dates + wide, FIELDS):
            out_ref[pl.ds(4 * g * 2 * FIELDS + f, 8, stride=FIELDS), :] = offsets_row


def solve_kernel(recv_ref, coh_ref, disp_ref, weight_ref, p_ref, r_ref, x_ref, q_ref, *, dates):
    quarters = recv_ref.shape[0] // (8 * FIELDS)
    chunk = 2 * FIELDS
    sub = rows_of((8, LANES))
    zero = jnp.zeros((8, LANES), F32)

    def received(quarter, f):
        return recv_ref[pl.ds(quarter * 8 * FIELDS + f, 8, stride=FIELDS), :]

    for d in range(4 * quarters):
        for row in range(2):
            coh_ref[pl.ds(d * 2 * K * dates + row, K * dates, stride=2), :] = recv_ref[
                pl.ds(d * chunk + row * FIELDS, K * dates), :
            ]

    def one_block_later(get, quarter):
        near = pltpu.roll(get(quarter), 6, 0)
        far = pltpu.roll(get(quarter + 1), 6, 0) if quarter + 1 < quarters else zero
        return jnp.where(sub < 6, near, far)

    def one_block_earlier(get, quarter):
        near = pltpu.roll(get(quarter), 2, 0)
        far = pltpu.roll(get(quarter - 1), 2, 0) if quarter > 0 else zero
        return jnp.where(sub >= 2, near, far)

    def over_dates(v):
        v = v + pltpu.roll(v, 4, 0)
        return v + pltpu.roll(v, 2, 0)

    def refresh_ghosts():
        for quarter in range(quarters):
            for e in range(SPAN):
                p_ref[quarter, SPAN + dates + e] = one_block_later(
                    lambda n: p_ref[n, SPAN + e], quarter
                )
                p_ref[quarter, e] = one_block_earlier(lambda n: p_ref[n, dates + e], quarter)

    rr = zero
    for quarter in range(quarters):
        offsets = received(quarter, K * dates + dates + SPAN)
        for u in range(dates):
            values = [received(quarter, K * u + k) for k in range(K)]
            places = [
                jnp.broadcast_to(offsets[:, K * u + k : K * u + k + 1], (8, LANES)) for k in range(K)
            ]
            for s in range(1, SPAN + 1):
                weight = zero
                for k in range(K):
                    weight = jnp.where(places[k] == float(s), values[k], weight)
                weight_ref[s - 1, quarter, SPAN + u] = weight
            b = received(quarter, K * dates + u)
            if u < SPAN:
                b = b + one_block_earlier(lambda n: received(n, K * dates + dates + u), quarter)
            p_ref[quarter, SPAN + u] = b
            r_ref[quarter, u] = b
            x_ref[pl.ds((quarter * dates + u) * 8, 8), :] = zero
            rr = rr + b * b
    for quarter in range(quarters):
        for s in range(1, SPAN + 1):
            for e in range(SPAN - s, SPAN):
                weight_ref[s - 1, quarter, e] = one_block_earlier(
                    lambda n: weight_ref[s - 1, n, dates + e], quarter
                )
    rr = over_dates(rr)
    refresh_ghosts()

    def iteration(step, rr):
        pq = zero
        for quarter in range(quarters):
            flows = {}
            for e in range(dates + SPAN):
                here = p_ref[quarter, e]
                out = None
                for s in range(1, SPAN + 1):
                    if e >= SPAN - s:
                        flow = weight_ref[s - 1, quarter, e] * (p_ref[quarter, e + s] - here)
                        flows[s, e] = flow
                        if e >= SPAN:
                            term = flows.pop((s, e - s)) - flow
                            out = term if out is None else out + term
                if e >= SPAN:
                    out = out + DAMPING * here
                    q_ref[quarter, e - SPAN] = out
                    pq = pq + here * out
        a = rr / (over_dates(pq) + EPSILON)
        nn = zero
        for quarter in range(quarters):
            for u in range(dates):
                rows = pl.ds((quarter * dates + u) * 8, 8)
                x_ref[rows, :] = x_ref[rows, :] + a * p_ref[quarter, SPAN + u]
                rest = r_ref[quarter, u] - a * q_ref[quarter, u]
                r_ref[quarter, u] = rest
                nn = nn + rest * rest
        nn = over_dates(nn)
        ratio = nn / (rr + EPSILON)
        for quarter in range(quarters):
            for u in range(dates):
                p_ref[quarter, SPAN + u] = r_ref[quarter, u] + ratio * p_ref[quarter, SPAN + u]
        refresh_ghosts()
        return nn

    lax.fori_loop(0, ITERS, iteration, rr)
    for quarter in range(quarters):
        for j in range(4):
            for row in range(2):
                disp_ref[pl.ds((quarter * 4 + j) * 2 * dates + row, dates, stride=2), :] = x_ref[
                    pl.ds(quarter * dates * 8 + 2 * j + row, dates, stride=8), :
                ]


def vmem(count):
    return [pl.BlockSpec(memory_space=pltpu.VMEM)] * count


PARAMS = pltpu.CompilerParams(vmem_limit_bytes=48 * 1024 * 1024)


def local(acquisitions, offsets):
    dates = acquisitions.shape[1]
    blocks = lax.axis_size("date")
    tiles = lax.axis_size("pix")
    packed, rim, corner = pl.pallas_call(
        pack_kernel,
        out_shape=[
            jax.ShapeDtypeStruct((dates, 8, LANES), F32),
            jax.ShapeDtypeStruct((2, SPAN, ROWS, LANES), F32),
            jax.ShapeDtypeStruct((SPAN, 8, LANES), F32),
        ],
        in_specs=vmem(1),
        out_specs=vmem(3),
        compiler_params=PARAMS,
    )(acquisitions)

    def moved(x, dates_back, tiles_on):
        route = [
            (p * blocks + d, (p + tiles_on) * blocks + d - dates_back)
            for p in range(tiles)
            for d in range(blocks)
            if 0 <= p + tiles_on < tiles and d >= dates_back
        ]
        return lax.ppermute(x, ("pix", "date"), route)

    left = moved(packed, 0, 1)
    right = moved(packed, 0, -1)
    rim = moved(rim, 1, 0)
    corner_left = moved(corner, 1, 1)
    corner_right = moved(corner, 1, -1)

    wide = dates + SPAN
    messages = pl.pallas_call(
        functools.partial(pair_kernel, batch=3),
        out_shape=jax.ShapeDtypeStruct((blocks * 2 * FIELDS, LANES), F32),
        in_specs=[pl.BlockSpec(memory_space=pltpu.SMEM)] + vmem(6),
        out_specs=vmem(1)[0],
        scratch_shapes=[
            pltpu.VMEM((2, wide, ROWS, LANES), F32),
            pltpu.VMEM((wide, 8, LANES), F32),
            pltpu.VMEM((wide, 8, LANES), F32),
            pltpu.VMEM((wide, ROWS, LANES), F32),
            pltpu.VMEM((wide, ROWS, LANES), F32),
        ],
        compiler_params=PARAMS,
    )(offsets, acquisitions, rim, left, right, corner_left, corner_right)
    received = lax.all_to_all(messages, "date", split_axis=0, concat_axis=0, tiled=True)

    quarters = blocks // 4
    coherence, displacement = pl.pallas_call(
        functools.partial(solve_kernel, dates=dates),
        out_shape=[
            jax.ShapeDtypeStruct((blocks * dates * K * 2, LANES), F32),
            jax.ShapeDtypeStruct((blocks * dates * 2, LANES), F32),
        ],
        in_specs=vmem(1),
        out_specs=vmem(2),
        scratch_shapes=[
            pltpu.VMEM((SPAN, quarters, SPAN + dates, 8, LANES), F32),
            pltpu.VMEM((quarters, dates + 2 * SPAN, 8, LANES), F32),
            pltpu.VMEM((quarters, dates, 8, LANES), F32),
            pltpu.VMEM((quarters * dates * 8, LANES), F32),
            pltpu.VMEM((quarters, dates, 8, LANES), F32),
        ],
        compiler_params=PARAMS,
    )(received)
    return (
        coherence.reshape(blocks * dates, K, 2, LANES),
        displacement.reshape(blocks * dates, 2, LANES),
    )


def solution(mesh):
    placed = (P(None, "date", None, "pix"), P("date", None))
    return jax.shard_map(
        local,
        mesh=mesh,
        in_specs=placed,
        out_specs=(P(None, None, "date", "pix"), P(None, "date", "pix")),
        check_vma=False,
    )
```

profile of v0, /device:TPU:32, one launch (start us, length us, event | category | flops | bytes accessed | tf_op | source)
XLA Modules:
  0.0 56.9 jit_solution(5697638185380198428)
XLA Ops:
  0.6 0.0 copy-start
  0.6 1.1 %copy-done = f32[2,18,32,128]{3,2,1,0:T(8,128)S(1)} copy-done((f32[2,18,32,128]{3,2,1,0:T(8,128)S(1)}, f32[2,18,32,128]{3,2,1,0:T(8,128)}, u32[]{:S(2)}) %copy-start) | copy-done | bytes 589848
  1.7 0.2 shard_map.41
  1.9 1.3 %collective-permute-start = (f32[2,4,32,128]{3,2,1,0:T(8,128)S(1)}, f32[2,4,32,128]{3,2,1,0:T(8,128)S(1)}, u32[]{:S(2)}, u32[]{:S(2)}) collective-permute-start(f32[2,4,32,128]{3,2,1,0:T(8,128)S(1)} %get-tuple-element.7), channel_id=1, source_target_pairs={{1,0},{2,1},{3,2},{4,3},{5,4},{6,5},{7,6},{8,7},{9,8},{10,9},{11,1... | collective-permute-start | bytes 393224 | tf_op jit(solution)/shard_map/ppermute | solution.py:325
  3.2 1.9 %collective-permute-start.2 = (f32[18,8,128]{2,1,0:T(8,128)S(1)}, f32[18,8,128]{2,1,0:T(8,128)S(1)}, u32[]{:S(2)}, u32[]{:S(2)}) collective-permute-start(f32[18,8,128]{2,1,0:T(8,128)S(1)} %get-tuple-element.8), channel_id=1, source_target_pairs={{16,0},{17,1},{18,2},{19,3},{20,4},{21,5},{22,6},{23,7},{24,8},{25... | collective-permute-start | bytes 221192 | tf_op jit(solution)/shard_map/ppermute | solution.py:325
  5.1 2.4 %collective-permute-start.1 = (f32[18,8,128]{2,1,0:T(8,128)S(1)}, f32[18,8,128]{2,1,0:T(8,128)S(1)}, u32[]{:S(2)}, u32[]{:S(2)}) collective-permute-start(f32[18,8,128]{2,1,0:T(8,128)S(1)} %get-tuple-element.8), channel_id=1, source_target_pairs={{0,16},{1,17},{2,18},{3,19},{4,20},{5,21},{6,22},{7,23},{8,24},{9,... | collective-permute-start | bytes 221192 | tf_op jit(solution)/shard_map/ppermute | solution.py:325
  7.6 1.3 %collective-permute-start.4 = (f32[4,8,128]{2,1,0:T(8,128)S(1)}, f32[4,8,128]{2,1,0:T(8,128)S(1)}, u32[]{:S(2)}, u32[]{:S(2)}) collective-permute-start(f32[4,8,128]{2,1,0:T(8,128)S(1)} %get-tuple-element.9), channel_id=1, source_target_pairs={{17,0},{18,1},{19,2},{20,3},{21,4},{22,5},{23,6},{24,7},{25,8},{26... | collective-permute-start | bytes 49160 | tf_op jit(solution)/shard_map/ppermute | solution.py:325
  8.9 1.3 %collective-permute-start.3 = (f32[4,8,128]{2,1,0:T(8,128)S(1)}, f32[4,8,128]{2,1,0:T(8,128)S(1)}, u32[]{:S(2)}, u32[]{:S(2)}) collective-permute-start(f32[4,8,128]{2,1,0:T(8,128)S(1)} %get-tuple-element.9), channel_id=1, source_target_pairs={{1,16},{2,17},{3,18},{4,19},{5,20},{6,21},{7,22},{8,23},{9,24},{10... | collective-permute-start | bytes 49160 | tf_op jit(solution)/shard_map/ppermute | solution.py:325
  10.2 0.8 %copy.4.off_ref = s32[18,3]{1,0:T(8,128)S(1)} copy(s32[18,3]{0,1:T(4,128)} %param.3) | data formatting | bytes 432 | tf_op args[1]
  10.9 3.7 %collective-permute-done.4.corner_right_ref = f32[4,8,128]{2,1,0:T(8,128)S(1)} collective-permute-done((f32[4,8,128]{2,1,0:T(8,128)S(1)}, f32[4,8,128]{2,1,0:T(8,128)S(1)}, u32[]{:S(2)}, u32[]{:S(2)}) %collective-permute-start.4) | collective-permute-done | bytes 16416 | tf_op jit(solution)/shard_map/ppermute | solution.py:325
  14.7 1.5 %collective-permute-done.3.corner_left_ref = f32[4,8,128]{2,1,0:T(8,128)S(1)} collective-permute-done((f32[4,8,128]{2,1,0:T(8,128)S(1)}, f32[4,8,128]{2,1,0:T(8,128)S(1)}, u32[]{:S(2)}, u32[]{:S(2)}) %collective-permute-start.3) | collective-permute-done | bytes 16416 | tf_op jit(solution)/shard_map/ppermute | solution.py:325
  16.1 0.0 collective-permute-done.2.right_ref
  16.1 0.0 collective-permute-done.1.left_ref
  16.1 0.0 collective-permute-done.rim_ref
  16.1 0.0 copy-start.1
  16.2 1.1 %copy-done.1 = f32[2,18,32,128]{3,2,1,0:T(8,128)S(1)} copy-done((f32[2,18,32,128]{3,2,1,0:T(8,128)S(1)}, f32[2,18,32,128]{3,2,1,0:T(8,128)}, u32[]{:S(2)}) %copy-start.1) | copy-done | bytes 589848
  17.2 5.4 %shard_map.42 = f32[2560,128]{1,0:T(8,128)S(1)} custom-call(s32[18,3]{1,0:T(8,128)S(1)} %copy.4.off_ref, f32[2,18,32,128]{3,2,1,0:T(8,128)S(1)} %copy-done.1, f32[2,4,32,128]{3,2,1,0:T(8,128)S(1)} %collective-permute-done.rim_ref, f32[18,8,128]{2,1,0:T(8,128)S(1)} %collective-permute-done.1.left_ref, f32[18,8,128]{2,1,0:T(8,128)S(1)} %collective-permute-done.2.right_ref, ...), custom_call_target="tpu_custom_call" | custom-call | tf_op jit(solution)/shard_map/pallas_call | solution.py:334
  22.7 30.5 %all_to_all.11 = f32[16,160,128]{2,1,0:T(8,128)S(1)} all-to-all(f32[16,160,128]{2,1,0:T(8,128)S(1)} %bitcast.4), channel_id=1, replica_groups=mesh['pix'=8,'date'=16] {'date'}, dimensions={0} | all-to-all | bytes 2621440 | tf_op jit(solution)/shard_map/all_to_all | solution.py:348
  53.2 3.7 %shard_map.43 = (f32[1728,128]{1,0:T(8,128)}, f32[576,128]{1,0:T(8,128)}) custom-call(f32[2560,128]{1,0:T(8,128)S(1)} %bitcast.5), custom_call_target="tpu_custom_call" | custom-call | tf_op jit(solution)/shard_map/pallas_call | solution.py:351
Async XLA Ops:
  0.6 1.1 %copy-start = (f32[2,18,32,128]{3,2,1,0:T(8,128)S(1)}, f32[2,18,32,128]{3,2,1,0:T(8,128)}, u32[]{:S(2)}) copy-start(f32[2,18,32,128]{3,2,1,0:T(8,128)} %acq_ref.3) | copy-start | bytes 1769476
  1.9 14.2 %collective-permute-start = (f32[2,4,32,128]{3,2,1,0:T(8,128)S(1)}, f32[2,4,32,128]{3,2,1,0:T(8,128)S(1)}, u32[]{:S(2)}, u32[]{:S(2)}) collective-permute-start(f32[2,4,32,128]{3,2,1,0:T(8,128)S(1)} %get-tuple-element.7), channel_id=1, source_target_pairs={{1,0},{2,1},{3,2},{4,3},{5,4},{6,5},{7,6},{8,7},{9,8},{10,9},{11,1... | collective-permute-start | bytes 393224 | tf_op jit(solution)/shard_map/ppermute | solution.py:325
  3.2 12.9 %collective-permute-start.2 = (f32[18,8,128]{2,1,0:T(8,128)S(1)}, f32[18,8,128]{2,1,0:T(8,128)S(1)}, u32[]{:S(2)}, u32[]{:S(2)}) collective-permute-start(f32[18,8,128]{2,1,0:T(8,128)S(1)} %get-tuple-element.8), channel_id=1, source_target_pairs={{16,0},{17,1},{18,2},{19,3},{20,4},{21,5},{22,6},{23,7},{24,8},{25... | collective-permute-start | bytes 221192 | tf_op jit(solution)/shard_map/ppermute | solution.py:325
  5.1 11.0 %collective-permute-start.1 = (f32[18,8,128]{2,1,0:T(8,128)S(1)}, f32[18,8,128]{2,1,0:T(8,128)S(1)}, u32[]{:S(2)}, u32[]{:S(2)}) collective-permute-start(f32[18,8,128]{2,1,0:T(8,128)S(1)} %get-tuple-element.8), channel_id=1, source_target_pairs={{0,16},{1,17},{2,18},{3,19},{4,20},{5,21},{6,22},{7,23},{8,24},{9,... | collective-permute-start | bytes 221192 | tf_op jit(solution)/shard_map/ppermute | solution.py:325
  7.6 7.1 %collective-permute-start.4 = (f32[4,8,128]{2,1,0:T(8,128)S(1)}, f32[4,8,128]{2,1,0:T(8,128)S(1)}, u32[]{:S(2)}, u32[]{:S(2)}) collective-permute-start(f32[4,8,128]{2,1,0:T(8,128)S(1)} %get-tuple-element.9), channel_id=1, source_target_pairs={{17,0},{18,1},{19,2},{20,3},{21,4},{22,5},{23,6},{24,7},{25,8},{26... | collective-permute-start | bytes 49160 | tf_op jit(solution)/shard_map/ppermute | solution.py:325
  8.9 7.3 %collective-permute-start.3 = (f32[4,8,128]{2,1,0:T(8,128)S(1)}, f32[4,8,128]{2,1,0:T(8,128)S(1)}, u32[]{:S(2)}, u32[]{:S(2)}) collective-permute-start(f32[4,8,128]{2,1,0:T(8,128)S(1)} %get-tuple-element.9), channel_id=1, source_target_pairs={{1,16},{2,17},{3,18},{4,19},{5,20},{6,21},{7,22},{8,23},{9,24},{10... | collective-permute-start | bytes 49160 | tf_op jit(solution)/shard_map/ppermute | solution.py:325
  16.1 1.1 %copy-start.1 = (f32[2,18,32,128]{3,2,1,0:T(8,128)S(1)}, f32[2,18,32,128]{3,2,1,0:T(8,128)}, u32[]{:S(2)}) copy-start(f32[2,18,32,128]{3,2,1,0:T(8,128)} %acq_ref.3) | copy-start | bytes 1769476
where the time goes:
time: 57.2 us; the launch traced here: 56.9 us
  blocking collectives  30.5 us (53%)
  Pallas kernels  9.31 us (16%)
  starting transfers between devices  8.2 us (14%)
  waiting for transfers between devices  5.21 us (9%)
  local copies, waits for them, and re-layouts  2.89 us (5%)
  between operations  0.7 us (1%)
    all_to_all x1, blocking collectives, local(): lax.all_to_all(messages, 'date', split_axis=0, concat_axis=0, tiled=True)  30.5 us
    ppermute x5, starting transfers between devices, moved(): return lax.ppermute(x, ('pix', 'date'), route)  8.2 us
    pallas_call x1, Pallas kernels, local(): pl.pallas_call(functools.partial(pair_kernel, batch=3), out_shape=jax.Sha...  5.44 us
    ppermute x5, waiting for transfers between devices, moved(): return lax.ppermute(x, ('pix', 'date'), route)  5.21 us
    pallas_call x1, Pallas kernels, local(): pl.pallas_call(functools.partial(solve_kernel, dates=dates), out_shape=[j...  3.66 us
    unnamed x5, local copies, waits for them, and re-layouts  2.89 us
  transfers between devices with their start and end apart: 5, of which 2 were waited for; matrix products, arithmetic and copies ran while one was open for 1% of the time, Pallas kernels for 0%

commit v1 on v0

--- a/solution.py
+++ b/solution.py
@@ -31,21 +31,29 @@
     return lax.broadcasted_iota(jnp.int32, shape, len(shape) - 2)
 
 
-def pack_kernel(acq_ref, packed_ref, rim_ref, corner_ref):
-    dates = acq_ref.shape[1]
+def pack_kernel(acq_ref, packed_ref, kept_ref, rim_ref):
     lane = lanes_of((8, LANES))
-    keep = (lane % 16) < 14
-    for t in range(dates):
+    for t in range(acq_ref.shape[1]):
         total = jnp.zeros((8, LANES), F32)
         for f in range(2):
             for g in range(GROUPS):
                 begin = 64 * f + 16 * g
-                moved = pltpu.roll(acq_ref[f, t, 8 * g : 8 * g + 8, :], begin + HC, 1)
-                total = jnp.where((lane >= begin) & (lane < begin + 14), moved, total)
+                here = acq_ref[f, t, 8 * g : 8 * g + 8, :]
+                kept_ref[f, t, 8 * g : 8 * g + 8, :] = here
+                if t < SPAN:
+                    rim_ref[f, t, 8 * g : 8 * g + 8, :] = here
+                moved = pltpu.roll(here, begin + HC, 1)
+                total = jnp.where((lane >= begin) & (lane < begin + 2 * HC), moved, total)
         packed_ref[t] = total
-        if t < SPAN:
-            corner_ref[t] = total
-    rim_ref[...] = acq_ref[:, :SPAN]
+
+
+def edges(left, right):
+    tile, tiles = lax.axis_index("pix"), lax.axis_size("pix")
+    lane = lanes_of(left.shape) % 16
+    low = jnp.where(tile == 0, HC, 0)
+    high = jnp.where(tile == tiles - 1, HC, 2 * HC)
+    both = jnp.where(lane < HC, left, right)
+    return jnp.where((lane >= low) & (lane < high), both, 0.0)
 
 
 def thirds(values):
@@ -73,113 +81,232 @@
     return [a + b + c for a, b, c in zip(parts, up(two, 1), down(two, 2, above))]
 
 
-def pair_kernel(
-    off_ref, acq_ref, rim_ref, left_ref, right_ref, corner_left_ref, corner_right_ref,
-    out_ref, ext_ref, halo_ref, turned_ref, power_ref, right_side_ref, *, batch,
-):
-    dates = acq_ref.shape[1]
-    total_dates = dates * lax.axis_size("date")
-    first = lax.axis_index("date") * dates
-    wide = dates + SPAN
-
+def center_band():
     row = lax.broadcasted_iota(jnp.int32, (LANES, LANES), 0)
     col = lax.broadcasted_iota(jnp.int32, (LANES, LANES), 1)
     band = (jnp.abs(row - col) <= HC).astype(F32).astype(BF16)
-    center_band = jnp.concatenate([band] * 3, axis=0)
+    return jnp.concatenate([band] * 3, axis=0)
+
+
+def halo_band():
+    row = lax.broadcasted_iota(jnp.int32, (LANES, LANES), 0)
+    col = lax.broadcasted_iota(jnp.int32, (LANES, LANES), 1)
     place = row % 16
     reach = ((place < HC) & (col <= place)) | (
         (place >= HC) & (place < 2 * HC) & (col >= LANES - 2 * HC + place)
     )
-    halo_band = jnp.concatenate(
+    band = jnp.concatenate(
         [(reach & ((row % 64) // 16 == g)).astype(F32).astype(BF16) for g in range(GROUPS)], axis=1
     )
-    halo_band = jnp.concatenate([halo_band] * 3, axis=0)
-
-    ext_ref[:, :dates] = acq_ref[...]
-    ext_ref[:, dates:] = rim_ref[...]
-    lane = lanes_of((8, LANES))
-    from_left = (lane % 16) < HC
-    sign = jnp.where(lane < 64, -1.0, 1.0).astype(F32)
-    for t in range(wide):
-        if t < dates:
-            halo = jnp.where(from_left, left_ref[t], right_ref[t])
-        else:
-            halo = jnp.where(from_left, corner_left_ref[t - dates], corner_right_ref[t - dates])
-        halo_ref[t] = halo
-        turned_ref[t] = pltpu.roll(halo, 64, 1) * sign
-        right_side_ref[t] = jnp.zeros((ROWS, LANES), F32)
-
-    def windows(products, halos):
-        n = len(products)
-        cols = jnp.dot(
-            thirds(jnp.concatenate(products, axis=0)), center_band, preferred_element_type=F32
+    return jnp.concatenate([band] * 3, axis=0)
+
+
+def banded(fields, band):
+    return jnp.dot(thirds(jnp.concatenate(fields, axis=0)), band, preferred_element_type=F32)
+
+
+def products(first, second):
+    (re, im), (re2, im2) = first, second
+    return [re * re2 + im * im2, im * re2 - re * im2]
+
+
+def turn(halo):
+    sign = jnp.where(lanes_of((8, LANES)) < 64, -1.0, 1.0).astype(F32)
+    return pltpu.roll(halo, 64, 1) * sign
+
+
+def windows(column_sums, halos, band):
+    rims = banded(halos, band)
+    return [
+        row_window(
+            [
+                column_sums(i, g) + rims[8 * i : 8 * i + 8, LANES * g : LANES * (g + 1)]
+                for g in range(GROUPS)
+            ]
         )
-        rims = jnp.dot(
-            thirds(jnp.concatenate(halos, axis=0)), halo_band, preferred_element_type=F32
-        )
-        return [
-            row_window(
-                [
-                    cols[ROWS * i + 8 * g : ROWS * i + 8 * g + 8]
-                    + rims[8 * i : 8 * i + 8, LANES * g : LANES * (g + 1)]
-                    for g in range(GROUPS)
-                ]
-            )
-            for i in range(n)
-        ]
-
-    per = 11
+        for i in range(len(halos))
+    ]
+
+
+def center_kernel(off_in, acq_ref, sums_ref, off_ref, sem, *, near, batch):
+    dates = acq_ref.shape[1]
+    copy = pltpu.make_async_copy(off_in, off_ref, sem)
+    copy.start()
+    band = center_band()
+
     def power_step(step, carry):
-        products, halos = [], []
-        for i in range(per):
-            t = step * per + i
-            re, im = ext_ref[0, t], ext_ref[1, t]
-            products.append(re * re + im * im)
-            halos.append(halo_ref[t] * halo_ref[t])
-        for i, parts in enumerate(windows(products, halos)):
-            t = step * per + i
-            for g in range(GROUPS):
-                power_ref[t, 8 * g : 8 * g + 8, :] = parts[g]
+        fields = []
+        for i in range(dates // 2):
+            re, im = acq_ref[0, step * (dates // 2) + i], acq_ref[1, step * (dates // 2) + i]
+            fields.append(re * re + im * im)
+        cols = banded(fields, band)
+        for i in range(dates // 2):
+            sums_ref[2 * K * near + step * (dates // 2) + i] = cols[ROWS * i : ROWS * (i + 1)]
         return carry
 
-    lax.fori_loop(0, wide // per, power_step, 0)
-
-    def pair_step(step, offsets_row):
-        products, halos, seconds = [], [], []
+    lax.fori_loop(0, 2, power_step, 0)
+
+    copy.wait()
+
+    def pair_step(step, carry):
+        fields = []
         for i in range(batch):
             t = step * batch + i
-            re, im, halo = ext_ref[0, t], ext_ref[1, t], halo_ref[t]
+            first = acq_ref[0, t], acq_ref[1, t]
             for k in range(K):
-                offset = off_ref[t, k]
-                j = t + offset
-                seconds.append((t, k, offset, j))
-                re2, im2 = ext_ref[0, j], ext_ref[1, j]
-                products.append(re * re2 + im * im2)
-                products.append(im * re2 - re * im2)
-                halos.append(halo * halo_ref[j])
-                halos.append(halo * turned_ref[j])
-        looked = windows(products, halos)
-        for n, (t, k, offset, j) in enumerate(seconds):
-            offsets_row = jnp.where(lane == K * t + k, offset.astype(F32), offsets_row)
-            usable = jnp.where(first + j < total_dates, 1.0, 0.0).astype(F32)
+                j = t + off_ref[k, t]
+                fields += products(first, (acq_ref[0, j], acq_ref[1, j]))
+        cols = banded(fields, band)
+        for i in range(2 * K * batch):
+            sums_ref[2 * K * batch * step + i] = cols[ROWS * i : ROWS * (i + 1)]
+        return carry
+
+    lax.fori_loop(0, near // batch, pair_step, 0)
+
+
+def finish_pair(looked, t, k, offset, usable, power_ref, out_ref, right_side_ref):
+    j = t + offset
+    for g in range(GROUPS):
+        rows = pl.ds(8 * g, 8)
+        re, im = looked[0][g], looked[1][g]
+        scale = lax.rsqrt(power_ref[t, rows, :] * power_ref[j, rows, :] + EPSILON)
+        if usable is not None:
+            scale = usable * scale
+        coherence = jnp.sqrt(re * re + im * im) * scale
+        flow = coherence * (im * scale)
+        out_ref[pl.ds(8 * g * FIELDS + K * t + k, 8, stride=FIELDS), :] = coherence
+        right_side_ref[t, rows, :] = right_side_ref[t, rows, :] - flow
+        right_side_ref[j, rows, :] = right_side_ref[j, rows, :] + flow
+
+
+def near_kernel(
+    off_in, acq_ref, rim_ref, left_ref, right_ref, sums_ref,
+    out_ref, halo_ref, power_ref, right_side_ref, far_sums_ref, turned_ref, next_ref, off_ref, sem, *, near, batch,
+):
+    dates = acq_ref.shape[1]
+    copy = pltpu.make_async_copy(off_in, off_ref, sem)
+    copy.start()
+    band = halo_band()
+    for t in range(dates + SPAN):
+        right_side_ref[t] = jnp.zeros((ROWS, LANES), F32)
+    for t in range(dates):
+        halo = edges(left_ref[t], right_ref[t])
+        halo_ref[t] = halo
+        turned_ref[t] = turn(halo)
+
+    half = dates // 2
+
+    def power_step(step, carry):
+        halos = [halo_ref[step * half + i] * halo_ref[step * half + i] for i in range(half)]
+
+        def column_sums(i, g):
+            return sums_ref[2 * K * near + step * half + i, 8 * g : 8 * g + 8, :]
+
+        for i, parts in enumerate(windows(column_sums, halos, band)):
             for g in range(GROUPS):
-                rows = pl.ds(8 * g, 8)
-                re, im = looked[2 * n][g], looked[2 * n + 1][g]
-                scale = usable * lax.rsqrt(power_ref[t, rows, :] * power_ref[j, rows, :] + EPSILON)
-                coherence = jnp.sqrt(re * re + im * im) * scale
-                flow = coherence * (im * scale)
-                out_ref[pl.ds(4 * g * 2 * FIELDS + K * t + k, 8, stride=FIELDS), :] = coherence
-                right_side_ref[t, rows, :] = right_side_ref[t, rows, :] - flow
-                right_side_ref[j, rows, :] = right_side_ref[j, rows, :] + flow
-        return offsets_row
-
-    offsets_row = lax.fori_loop(0, dates // batch, pair_step, jnp.zeros((8, LANES), F32))
+                power_ref[step * half + i, 8 * g : 8 * g + 8, :] = parts[g]
+        return carry
+
+    lax.fori_loop(0, 2, power_step, 0)
+
+    copy.wait()
+
+    def pair_step(step, carry):
+        halos, pairs = [], []
+        for i in range(batch):
+            t = step * batch + i
+            halo = halo_ref[t]
+            for k in range(K):
+                offset = off_ref[k, t]
+                pairs.append((t, k, offset))
+                halos += [halo * halo_ref[t + offset], halo * turned_ref[t + offset]]
+
+        def column_sums(i, g):
+            return sums_ref[2 * K * batch * step + i, 8 * g : 8 * g + 8, :]
+
+        looked = windows(column_sums, halos, band)
+        for n, (t, k, offset) in enumerate(pairs):
+            finish_pair(
+                looked[2 * n : 2 * n + 2], t, k, offset, None, power_ref, out_ref, right_side_ref
+            )
+        return carry
+
+    lax.fori_loop(0, near // batch, pair_step, 0)
+
+    for t in range(near):
+        for g in range(GROUPS):
+            out_ref[pl.ds(8 * g * FIELDS + K * dates + t, 8, stride=FIELDS), :] = right_side_ref[
+                t, 8 * g : 8 * g + 8, :
+            ]
+
+    fields = []
+    last = lax.axis_index("date") == lax.axis_size("date") - 1
+    for t in range(SPAN):
+        for f in range(2):
+            next_ref[f, t] = jnp.where(last, 0.0, rim_ref[f, t])
+        re, im = next_ref[0, t], next_ref[1, t]
+        fields.append(re * re + im * im)
+    for t in range(near, dates):
+        first = acq_ref[0, t], acq_ref[1, t]
+        for k in range(K):
+            j = t + off_ref[k, t]
+            inside = j < dates
+            j_in, j_out = jnp.minimum(j, dates - 1), jnp.maximum(j - dates, 0)
+            second = [jnp.where(inside, acq_ref[f, j_in], next_ref[f, j_out]) for f in range(2)]
+            fields += products(first, second)
+    cols = banded(fields, center_band())
+    for i in range(len(fields)):
+        far_sums_ref[i] = cols[ROWS * i : ROWS * (i + 1)]
+
+
+def far_kernel(
+    off_in, message_ref, near_halo_ref, corner_ref, near_power_ref, near_right_ref, sums_ref,
+    out_ref, halo_ref, turned_ref, power_ref, right_side_ref, off_ref, sem, *, near,
+):
+    del message_ref
+    copy = pltpu.make_async_copy(off_in, off_ref, sem)
+    copy.start()
+    dates = near_halo_ref.shape[0]
+    total_dates = dates * lax.axis_size("date")
+    first = lax.axis_index("date") * dates
+    band = halo_band()
+    for t in range(near, dates + SPAN):
+        halo = near_halo_ref[t] if t < dates else corner_ref[t - dates]
+        halo_ref[t] = halo
+        turned_ref[t] = turn(halo)
+        right_side_ref[t] = near_right_ref[t]
+        if t < dates:
+            power_ref[t] = near_power_ref[t]
+
+    halos = [halo_ref[dates + t] * halo_ref[dates + t] for t in range(SPAN)]
+    powers = windows(lambda i, g: sums_ref[i, 8 * g : 8 * g + 8, :], halos, band)
+    for t in range(SPAN):
+        for g in range(GROUPS):
+            power_ref[dates + t, 8 * g : 8 * g + 8, :] = powers[t][g]
+    copy.wait()
+    pairs, halos = [], []
+    for t in range(near, dates):
+        for k in range(K):
+            offset = off_ref[k, t]
+            pairs.append((t, k, offset))
+            halos += [halo_ref[t] * halo_ref[t + offset], halo_ref[t] * turned_ref[t + offset]]
+    looked = windows(lambda i, g: sums_ref[SPAN + i, 8 * g : 8 * g + 8, :], halos, band)
+    for n, (t, k, offset) in enumerate(pairs):
+        usable = jnp.where(first + t + offset < total_dates, 1.0, 0.0).astype(F32)
+        finish_pair(
+            looked[2 * n : 2 * n + 2], t, k, offset, usable, power_ref, out_ref, right_side_ref
+        )
+    lane = lanes_of((8, LANES))
+    offsets_row = jnp.zeros((8, LANES), F32)
+    for t in range(dates):
+        for k in range(K):
+            offsets_row = jnp.where(lane == K * t + k, off_ref[k, t].astype(F32), offsets_row)
     for g in range(GROUPS):
-        base = 4 * g * 2 * FIELDS + K * dates
-        for t in range(wide):
+        base = 8 * g * FIELDS + K * dates
+        for t in range(near, dates + SPAN):
             out_ref[pl.ds(base + t, 8, stride=FIELDS), :] = right_side_ref[t, 8 * g : 8 * g + 8, :]
-        for f in range(K * dates + wide, FIELDS):
-            out_ref[pl.ds(4 * g * 2 * FIELDS + f, 8, stride=FIELDS), :] = offsets_row
+        for f in range(dates + SPAN, FIELDS - K * dates):
+            out_ref[pl.ds(base + f, 8, stride=FIELDS), :] = offsets_row
 
 
 def solve_kernel(recv_ref, coh_ref, disp_ref, weight_ref, p_ref, r_ref, x_ref, q_ref, *, dates):
@@ -299,52 +426,91 @@
 PARAMS = pltpu.CompilerParams(vmem_limit_bytes=48 * 1024 * 1024)
 
 
+def shape(*sizes):
+    return jax.ShapeDtypeStruct(sizes, F32)
+
+
 def local(acquisitions, offsets):
     dates = acquisitions.shape[1]
     blocks = lax.axis_size("date")
     tiles = lax.axis_size("pix")
-    packed, rim, corner = pl.pallas_call(
+    near, wide = dates - SPAN, dates + SPAN
+    anywhere = [pl.BlockSpec(memory_space=pl.ANY)]
+    table = [pltpu.SMEM((K, dates), jnp.int32), pltpu.SemaphoreType.DMA]
+    offsets = offsets.T
+    packed, kept, rim = pl.pallas_call(
         pack_kernel,
         out_shape=[
-            jax.ShapeDtypeStruct((dates, 8, LANES), F32),
-            jax.ShapeDtypeStruct((2, SPAN, ROWS, LANES), F32),
-            jax.ShapeDtypeStruct((SPAN, 8, LANES), F32),
+            shape(dates, 8, LANES), shape(2, dates, ROWS, LANES), shape(2, SPAN, ROWS, LANES)
         ],
         in_specs=vmem(1),
         out_specs=vmem(3),
         compiler_params=PARAMS,
     )(acquisitions)
 
-    def moved(x, dates_back, tiles_on):
-        route = [
-            (p * blocks + d, (p + tiles_on) * blocks + d - dates_back)
-            for p in range(tiles)
-            for d in range(blocks)
-            if 0 <= p + tiles_on < tiles and d >= dates_back
-        ]
-        return lax.ppermute(x, ("pix", "date"), route)
-
-    left = moved(packed, 0, 1)
-    right = moved(packed, 0, -1)
-    rim = moved(rim, 1, 0)
-    corner_left = moved(corner, 1, 1)
-    corner_right = moved(corner, 1, -1)
-
-    wide = dates + SPAN
+    up = [(p, (p + 1) % tiles) for p in range(tiles)]
+    left = lax.ppermute(packed, "pix", up)
+    right = lax.ppermute(packed, "pix", [(j, i) for i, j in up])
+    back = [((d + 1) % blocks, d) for d in range(blocks)]
+    rim = lax.ppermute(rim, "date", back)
+
+    sums = pl.pallas_call(
+        functools.partial(center_kernel, near=near, batch=7),
+        out_shape=shape(2 * K * near + dates, ROWS, LANES),
+        in_specs=anywhere + vmem(1),
+        out_specs=vmem(1)[0],
+        scratch_shapes=table,
+        compiler_params=PARAMS,
+    )(offsets, kept)
+
+    def corner_kernel(left_ref, right_ref, sums_ref, out_ref):
+        del sums_ref
+        for t in range(SPAN):
+            out_ref[t] = edges(left_ref[t], right_ref[t])
+
+    corner = pl.pallas_call(
+        corner_kernel,
+        out_shape=shape(SPAN, 8, LANES),
+        in_specs=vmem(2) + anywhere,
+        out_specs=vmem(1)[0],
+        compiler_params=PARAMS,
+    )(left, right, sums)
+    corner = lax.ppermute(corner, "date", back)
+
+    messages, halo, power, right_side, far_sums = pl.pallas_call(
+        functools.partial(near_kernel, near=near, batch=7),
+        out_shape=[
+            shape(blocks * 2 * FIELDS, LANES),
+            shape(dates, 8, LANES),
+            shape(dates, ROWS, LANES),
+            shape(wide, ROWS, LANES),
+            shape(SPAN + 2 * K * SPAN, ROWS, LANES),
+        ],
+        in_specs=anywhere + vmem(5),
+        out_specs=vmem(5),
+        scratch_shapes=[
+            pltpu.VMEM((dates, 8, LANES), F32),
+            pltpu.VMEM((2, SPAN, ROWS, LANES), F32),
+            *table,
+        ],
+        compiler_params=PARAMS,
+    )(offsets, kept, rim, left, right, sums)
+
     messages = pl.pallas_call(
-        functools.partial(pair_kernel, batch=3),
-        out_shape=jax.ShapeDtypeStruct((blocks * 2 * FIELDS, LANES), F32),
-        in_specs=[pl.BlockSpec(memory_space=pltpu.SMEM)] + vmem(6),
+        functools.partial(far_kernel, near=near),
+        out_shape=shape(blocks * 2 * FIELDS, LANES),
+        in_specs=anywhere + vmem(6),
         out_specs=vmem(1)[0],
+        input_output_aliases={1: 0},
         scratch_shapes=[
-            pltpu.VMEM((2, wide, ROWS, LANES), F32),
             pltpu.VMEM((wide, 8, LANES), F32),
             pltpu.VMEM((wide, 8, LANES), F32),
             pltpu.VMEM((wide, ROWS, LANES), F32),
             pltpu.VMEM((wide, ROWS, LANES), F32),
+            *table,
         ],
         compiler_params=PARAMS,
-    )(offsets, acquisitions, rim, left, right, corner_left, corner_right)
+    )(offsets, messages, halo, corner, power, right_side, far_sums)
     received = lax.all_to_all(messages, "date", split_axis=0, concat_axis=0, tiled=True)
 
     quarters = blocks // 4

time: 57.2 us -> 46.5 us (0.81)
  waiting for transfers between devices: 5.21 us -> 0.01 us
  blocking collectives: 30.5 us -> 26.1 us
  local copies, waits for them, and re-layouts: 2.89 us -> 1.74 us
    ppermute x5 -> x4, waiting for transfers between devices: 5.21 us -> 0.01 us  [the longest x1 0.01 us: local(): rim = lax.ppermute(rim, 'date', back)]
    all_to_all x1, blocking collectives: 30.5 us -> 26.1 us  [local(): lax.all_to_all(messages, 'date', split_axis=0, concat_axis=0, tiled=True)]
    unnamed x5 -> x4, local copies, waits for them, and re-layouts: 2.89 us -> 1.74 us
    pallas_call x2 -> x5, Pallas kernels: 5.65 us -> 6.12 us  [the longest x1 3.04 us: local(): pl.pallas_call(functools.partial(near_kernel, near=near, batch=7), out_sh...]
    ppermute x5 -> x4, starting transfers between devices: 8.2 us -> 7.91 us  [the longest x1 5.28 us: local(): rim = lax.ppermute(rim, 'date', back)]
  transfers between devices with their start and end apart: 5 -> 4, of which waited for: 2 -> 0; matrix products, arithmetic and copies ran while one was open for 1% -> 0% of each run, Pallas kernels for 0% -> 10%
where the time goes in v1:
time: 46.5 us; the launch traced here: 46.2 us
  blocking collectives  26.1 us (56%)
  Pallas kernels  9.75 us (21%)
  starting transfers between devices  7.91 us (17%)
  local copies, waits for them, and re-layouts  1.74 us (4%)
  between operations  0.7 us (2%)
    all_to_all x1, blocking collectives, local(): lax.all_to_all(messages, 'date', split_axis=0, concat_axis=0, tiled=True)  26.1 us
    ppermute x1, starting transfers between devices, local(): rim = lax.ppermute(rim, 'date', back)  5.28 us
    pallas_call x1, Pallas kernels, local(): pl.pallas_call(functools.partial(solve_kernel, dates=dates), out_shape=[j...  3.63 us
    pallas_call x1, Pallas kernels, local(): pl.pallas_call(functools.partial(near_kernel, near=near, batch=7), out_sh...  3.04 us
    ppermute x1, starting transfers between devices, local(): right = lax.ppermute(packed, 'pix', [(j, i) for i, j in up])  1.74 us
    unnamed x4, local copies, waits for them, and re-layouts  1.74 us
    pallas_call x1, Pallas kernels, local(): pl.pallas_call(functools.partial(center_kernel, near=near, batch=7), out_...  1.48 us
    pallas_call x1, Pallas kernels, local(): pl.pallas_call(functools.partial(far_kernel, near=near), out_shape=shape(...  1.36 us
  transfers between devices with their start and end apart: 4, of which 0 were waited for; matrix products, arithmetic and copies ran while one was open for 0% of the time, Pallas kernels for 10%

profile of v1, /device:TPU:32, one launch (start us, length us, event | category | flops | bytes accessed | tf_op | source)
XLA Modules:
  0.0 46.2 jit_solution(3891133521563782123)
XLA Ops:
  0.6 0.0 copy-start
  0.6 1.1 %copy-done = f32[2,18,32,128]{3,2,1,0:T(8,128)S(1)} copy-done((f32[2,18,32,128]{3,2,1,0:T(8,128)S(1)}, f32[2,18,32,128]{3,2,1,0:T(8,128)}, u32[]{:S(2)}) %copy-start) | copy-done | bytes 589848
  1.7 0.2 shard_map.41
  1.9 5.3 %collective-permute-start = (f32[2,4,32,128]{3,2,1,0:T(8,128)S(1)}, f32[2,4,32,128]{3,2,1,0:T(8,128)S(1)}, u32[]{:S(2)}, u32[]{:S(2)}) collective-permute-start(f32[2,4,32,128]{3,2,1,0:T(8,128)S(1)} %get-tuple-element.13), channel_id=1, source_target_pairs={{1,0},{2,1},{3,2},{4,3},{5,4},{6,5},{7,6},{8,7},{9,8},{10,9},{11,1... | collective-permute-start | bytes 393224 | tf_op jit(solution)/shard_map/ppermute | solution.py:455
  7.2 0.0 collective-permute-start.1
  7.2 1.7 %collective-permute-start.2 = (f32[18,8,128]{2,1,0:T(8,128)S(1)}, f32[18,8,128]{2,1,0:T(8,128)S(1)}, u32[]{:S(2)}, u32[]{:S(2)}) collective-permute-start(f32[18,8,128]{2,1,0:T(8,128)S(1)} %get-tuple-element.14), channel_id=1, source_target_pairs={{16,0},{32,16},{48,32},{64,48},{80,64},{96,80},{112,96},{0,112},{1... | collective-permute-start | bytes 221192 | tf_op jit(solution)/shard_map/ppermute | solution.py:453
  8.9 0.0 copy-start.1
  9.0 0.7 %copy-done.1 = s32[18,3]{0,1:T(4,128)S(1)} copy-done((s32[18,3]{0,1:T(4,128)S(1)}, s32[18,3]{0,1:T(4,128)}, u32[]{:S(2)}) %copy-start.1) | copy-done | bytes 240
  9.6 1.5 %shard_map.42.sums_ref = f32[102,32,128]{2,1,0:T(8,128)S(1)} custom-call(s32[3,18]{1,0:T(4,128)S(1)} %bitcast.7, f32[2,18,32,128]{3,2,1,0:T(8,128)S(1)} %get-tuple-element.12.acq_ref), custom_call_target="tpu_custom_call" | custom-call | tf_op jit(solution)/shard_map/pallas_call | solution.py:457
  11.1 0.0 collective-permute-done.1.left_ref
  11.1 0.0 collective-permute-done.2.right_ref
  11.2 0.9 %collective-permute-start.3 = (f32[4,8,128]{2,1,0:T(8,128)S(1)}, f32[4,8,128]{2,1,0:T(8,128)S(1)}, u32[]{:S(2)}, u32[]{:S(2)}) collective-permute-start(f32[4,8,128]{2,1,0:T(8,128)S(1)} %shard_map.44), channel_id=1, source_target_pairs={{1,0},{2,1},{3,2},{4,3},{5,4},{6,5},{7,6},{8,7},{9,8},{10,9},{11,1... | collective-permute-start | bytes 49160 | tf_op jit(solution)/shard_map/ppermute | solution.py:478
  12.1 0.0 collective-permute-done.rim_ref
  12.1 3.0 %shard_map.43 = (f32[2560,128]{1,0:T(8,128)S(1)}, f32[18,8,128]{2,1,0:T(8,128)S(1)}, f32[18,32,128]{2,1,0:T(8,128)S(1)}, f32[22,32,128]{2,1,0:T(8,128)S(1)}, f32[28,32,128]{2,1,0:T(8,128)S(1)}) custom-call(s32[3,18]{1,0:T(4,128)S(1)} %bitcast.8, f32[2,18,32,128]{3,2,1,0:T(8,128)S(1)} %get-tuple-element.12.acq_ref, ...), custom_call_target="tpu_custom_call" | custom-call | tf_op jit(solution)/shard_map/pallas_call | solution.py:480
  15.1 0.0 collective-permute-done.3.corner_ref
  15.1 1.4 %shard_map.45 = f32[2560,128]{1,0:T(8,128)S(1)} custom-call(s32[3,18]{1,0:T(4,128)S(1)} %bitcast.9, f32[2560,128]{1,0:T(8,128)S(1)} %get-tuple-element.15.message_ref, f32[18,8,128]{2,1,0:T(8,128)S(1)} %get-tuple-element.16.near_halo_ref, f32[4,8,128]{2,1,0:T(8,128)S(1)} %collective-permute-done.3.corner_ref, ...), custom_call_target="tpu_custom_call", output_to_operand_aliasing={{}: (1, {})} | custom-call | tf_op jit(solution)/shard_map/pallas_call | solution.py:499
  16.5 26.1 %all_to_all.11 = f32[16,160,128]{2,1,0:T(8,128)S(1)} all-to-all(f32[16,160,128]{2,1,0:T(8,128)S(1)} %bitcast.5), channel_id=1, replica_groups=mesh['pix'=8,'date'=16] {'date'}, dimensions={0} | all-to-all | bytes 2621440 | tf_op jit(solution)/shard_map/all_to_all | solution.py:514
  42.6 3.6 %shard_map.46 = (f32[1728,128]{1,0:T(8,128)}, f32[576,128]{1,0:T(8,128)}) custom-call(f32[2560,128]{1,0:T(8,128)S(1)} %bitcast.6), custom_call_target="tpu_custom_call" | custom-call | tf_op jit(solution)/shard_map/pallas_call | solution.py:517
  (1 shorter events, 0.0 us)
Async XLA Ops:
  0.6 1.1 %copy-start = (f32[2,18,32,128]{3,2,1,0:T(8,128)S(1)}, f32[2,18,32,128]{3,2,1,0:T(8,128)}, u32[]{:S(2)}) copy-start(f32[2,18,32,128]{3,2,1,0:T(8,128)} %acq_ref.1) | copy-start | bytes 1769476
  1.9 10.1 %collective-permute-start = (f32[2,4,32,128]{3,2,1,0:T(8,128)S(1)}, f32[2,4,32,128]{3,2,1,0:T(8,128)S(1)}, u32[]{:S(2)}, u32[]{:S(2)}) collective-permute-start(f32[2,4,32,128]{3,2,1,0:T(8,128)S(1)} %get-tuple-element.13), channel_id=1, source_target_pairs={{1,0},{2,1},{3,2},{4,3},{5,4},{6,5},{7,6},{8,7},{9,8},{10,9},{11,1... | collective-permute-start | bytes 393224 | tf_op jit(solution)/shard_map/ppermute | solution.py:455
  7.2 3.9 %collective-permute-start.1 = (f32[18,8,128]{2,1,0:T(8,128)S(1)}, f32[18,8,128]{2,1,0:T(8,128)S(1)}, u32[]{:S(2)}, u32[]{:S(2)}) collective-permute-start(f32[18,8,128]{2,1,0:T(8,128)S(1)} %get-tuple-element.14), channel_id=1, source_target_pairs={{0,16},{16,32},{32,48},{48,64},{64,80},{80,96},{96,112},{112,0},{1... | collective-permute-start | bytes 221192 | tf_op jit(solution)/shard_map/ppermute | solution.py:452
  7.2 3.9 %collective-permute-start.2 = (f32[18,8,128]{2,1,0:T(8,128)S(1)}, f32[18,8,128]{2,1,0:T(8,128)S(1)}, u32[]{:S(2)}, u32[]{:S(2)}) collective-permute-start(f32[18,8,128]{2,1,0:T(8,128)S(1)} %get-tuple-element.14), channel_id=1, source_target_pairs={{16,0},{32,16},{48,32},{64,48},{80,64},{96,80},{112,96},{0,112},{1... | collective-permute-start | bytes 221192 | tf_op jit(solution)/shard_map/ppermute | solution.py:453
  8.9 0.7 %copy-start.1 = (s32[18,3]{0,1:T(4,128)S(1)}, s32[18,3]{0,1:T(4,128)}, u32[]{:S(2)}) copy-start(s32[18,3]{0,1:T(4,128)} %param.3) | copy-start | bytes 652
  11.2 3.9 %collective-permute-start.3 = (f32[4,8,128]{2,1,0:T(8,128)S(1)}, f32[4,8,128]{2,1,0:T(8,128)S(1)}, u32[]{:S(2)}, u32[]{:S(2)}) collective-permute-start(f32[4,8,128]{2,1,0:T(8,128)S(1)} %shard_map.44), channel_id=1, source_target_pairs={{1,0},{2,1},{3,2},{4,3},{5,4},{6,5},{7,6},{8,7},{9,8},{10,9},{11,1... | collective-permute-start | bytes 49160 | tf_op jit(solution)/shard_map/ppermute | solution.py:478

commit v2 on v1

v2 whole, which is shorter than its diff:
```python
import functools

import jax
import jax.numpy as jnp
from jax import lax
from jax.experimental import pallas as pl
from jax.experimental.pallas import tpu as pltpu
from jax.sharding import PartitionSpec as P

SPAN = 4
K = 3
HR = 2
HC = 7
ITERS = 6
DAMPING = 0.05
EPSILON = 1e-06

LANES = 128
ROWS = 32
GROUPS = ROWS // 8
FIELDS = 76
F32 = jnp.float32
BF16 = jnp.bfloat16


def lanes_of(shape):
    return lax.broadcasted_iota(jnp.int32, shape, len(shape) - 1)


def rows_of(shape):
    return lax.broadcasted_iota(jnp.int32, shape, len(shape) - 2)


def pack_kernel(acq_ref, packed_ref, kept_ref, rim_ref):
    lane = lanes_of((8, LANES))
    for t in range(acq_ref.shape[1]):
        total = jnp.zeros((8, LANES), F32)
        for f in range(2):
            for g in range(GROUPS):
                begin = 64 * f + 16 * g
                here = acq_ref[f, t, 8 * g : 8 * g + 8, :]
                kept_ref[f, t, 8 * g : 8 * g + 8, :] = here
                if t < SPAN:
                    rim_ref[f, t, 8 * g : 8 * g + 8, :] = here
                moved = pltpu.roll(here, begin + HC, 1)
                total = jnp.where((lane >= begin) & (lane < begin + 2 * HC), moved, total)
        packed_ref[t] = total


def edges(left, right):
    tile, tiles = lax.axis_index("pix"), lax.axis_size("pix")
    lane = lanes_of(left.shape) % 16
    low = jnp.where(tile == 0, HC, 0)
    high = jnp.where(tile == tiles - 1, HC, 2 * HC)
    both = jnp.where(lane < HC, left, right)
    return jnp.where((lane >= low) & (lane < high), both, 0.0)


def halves(values):
    high = values.astype(BF16)
    return jnp.concatenate([high, (values - high.astype(F32)).astype(BF16)], axis=1)


def row_window(parts):
    sub = rows_of((8, LANES))
    zero = jnp.zeros((8, LANES), F32)

    def up(x, n, below):
        x = x + [below]
        return [pltpu.roll(jnp.where(sub >= n, x[g], x[g + 1]), 8 - n, 0) for g in range(GROUPS)]

    def down(x, n, above):
        x = [above] + x
        return [pltpu.roll(jnp.where(sub < 8 - n, x[g + 1], x[g]), n, 0) for g in range(GROUPS)]

    two = [a + b for a, b in zip(parts, up(parts, 1, zero))]
    above = jnp.where(sub == 7, pltpu.roll(parts[0], 7, 0), 0.0)
    return [a + b + c for a, b, c in zip(parts, up(two, 1, zero), down(two, 2, above))]


def packed_window(x):
    sub, place = rows_of((8, LANES)), lanes_of((8, LANES)) % 64
    below = jnp.where(place < 48, pltpu.roll(x, LANES - 16, 1), 0.0)
    above = jnp.where(place >= 16, pltpu.roll(x, 16, 1), 0.0)
    total = x
    for n in range(1, HR + 1):
        total = total + pltpu.roll(jnp.where(sub >= n, x, below), 8 - n, 0)
        total = total + pltpu.roll(jnp.where(sub < 8 - n, x, above), n, 0)
    return total


def center_band():
    row = lax.broadcasted_iota(jnp.int32, (LANES, LANES), 0)
    col = lax.broadcasted_iota(jnp.int32, (LANES, LANES), 1)
    band = (jnp.abs(row - col) <= HC).astype(F32).astype(BF16)
    return jnp.concatenate([band] * 2, axis=0)


def halo_band():
    row = lax.broadcasted_iota(jnp.int32, (LANES, LANES), 0)
    col = lax.broadcasted_iota(jnp.int32, (LANES, LANES), 1)
    place = row % 16
    reach = ((place < HC) & (col <= place)) | (
        (place >= HC) & (place < 2 * HC) & (col >= LANES - 2 * HC + place)
    )
    band = jnp.concatenate(
        [(reach & ((row % 64) // 16 == g)).astype(F32).astype(BF16) for g in range(GROUPS)], axis=1
    )
    return jnp.concatenate([band] * 2, axis=0)


def banded(fields, band):
    return jnp.dot(halves(jnp.concatenate(fields, axis=0)), band, preferred_element_type=F32)


def products(first, second):
    (re, im), (re2, im2) = first, second
    return [re * re2 + im * im2, im * re2 - re * im2]


def turn(halo):
    sign = jnp.where(lanes_of((8, LANES)) < 64, -1.0, 1.0).astype(F32)
    return pltpu.roll(halo, 64, 1) * sign


def center_windows(fields, band, out_ref, at):
    cols = banded(fields, band)
    for i in range(len(fields)):
        parts = [cols[ROWS * i + 8 * g : ROWS * i + 8 * g + 8] for g in range(GROUPS)]
        for g, part in enumerate(row_window(parts)):
            out_ref[at + i, 8 * g : 8 * g + 8, :] = part


def windows(center_ref, at, halos, band):
    rims = banded([packed_window(halo) for halo in halos], band)
    return [
        [
            center_ref[at + i, 8 * g : 8 * g + 8, :]
            + rims[8 * i : 8 * i + 8, LANES * g : LANES * (g + 1)]
            for g in range(GROUPS)
        ]
        for i in range(len(halos))
    ]


def chosen(offset, candidates):
    result = candidates[-1]
    for s in range(len(candidates) - 1, 0, -1):
        result = jnp.where(offset == float(s), candidates[s - 1], result)
    return result


def pair_fields(value, table_ref, dates):
    fields = []
    for t in dates:
        first = [[value(f, t, g) for f in range(2)] for g in range(GROUPS)]
        for k in range(K):
            offset = table_ref[K * t + k]
            pairs = [
                products(
                    first[g],
                    [
                        chosen(offset, [value(f, t + s, g) for s in range(1, SPAN + 1)])
                        for f in range(2)
                    ],
                )
                for g in range(GROUPS)
            ]
            fields += [jnp.concatenate([pair[c] for pair in pairs], axis=0) for c in range(2)]
    return fields


def power_fields(value, dates):
    fields = []
    for t in dates:
        parts = [[value(f, t, g) for f in range(2)] for g in range(GROUPS)]
        fields.append(jnp.concatenate([re * re + im * im for re, im in parts], axis=0))
    return fields


def center_kernel(off_ref, acq_ref, sums_ref, table_ref, *, near, batch):
    dates = acq_ref.shape[1]
    band = center_band()
    lane = lanes_of((8, LANES))
    row = jnp.zeros((8, LANES), F32)
    offsets = off_ref[...].astype(F32)
    for t in range(dates):
        for k in range(K):
            offset = jnp.broadcast_to(offsets[k : k + 1, t : t + 1], (8, LANES))
            table_ref[K * t + k] = offset
            row = jnp.where(lane == K * t + k, offset, row)
    table_ref[K * dates] = row

    def value(f, t, g):
        return acq_ref[f, t, 8 * g : 8 * g + 8, :]

    for begin in range(0, dates, dates // 2):
        fields = power_fields(value, range(begin, begin + dates // 2))
        center_windows(fields, band, sums_ref, 2 * K * near + begin)
    for begin in range(0, near, batch):
        fields = pair_fields(value, table_ref, range(begin, begin + batch))
        center_windows(fields, band, sums_ref, 2 * K * begin)


def far_center_kernel(table_ref, acq_ref, rim_ref, sums_ref, *, near):
    dates = acq_ref.shape[1]
    last = lax.axis_index("date") == lax.axis_size("date") - 1

    def value(f, t, g):
        rows = pl.ds(8 * g, 8)
        if t < dates:
            return acq_ref[f, t, rows, :]
        return jnp.where(last, 0.0, rim_ref[f, t - dates, rows, :])

    fields = power_fields(value, range(dates, dates + SPAN))
    fields += pair_fields(value, table_ref, range(near, dates))
    center_windows(fields, center_band(), sums_ref, 0)


def halo_pairs(table_ref, halo, turned, dates):
    fields = []
    for t in dates:
        for k in range(K):
            for field in (halo, turned):
                second = chosen(table_ref[K * t + k], [field(t + s) for s in range(1, SPAN + 1)])
                fields.append(halo(t) * second)
    return fields


def finish(looked, t, table_ref, power, limit, out_ref, add):
    offsets = [table_ref[K * t + k] for k in range(K)]
    for g in range(GROUPS):
        flows = []
        for k in range(K):
            re, im = looked[2 * k][g], looked[2 * k + 1][g]
            second = chosen(offsets[k], [power(t + s, g) for s in range(1, SPAN + 1)])
            scale = lax.rsqrt(power(t, g) * second + EPSILON)
            if limit is not None:
                scale = jnp.where(offsets[k] < limit, scale, 0.0)
            coherence = jnp.sqrt(re * re + im * im) * scale
            out_ref[pl.ds(8 * g * FIELDS + K * t + k, 8, stride=FIELDS), :] = coherence
            flows.append(coherence * (im * scale))
        total = flows[0]
        for flow in flows[1:]:
            total = total + flow
        add(t, g, -total)
        for s in range(1, SPAN + 1):
            share = jnp.zeros((8, LANES), F32)
            for offset, flow in zip(offsets, flows):
                share = jnp.where(offset == float(s), flow, share)
            add(t + s, g, share)


def near_kernel(
    table_ref, left_ref, right_ref, sums_ref,
    out_ref, halo_ref, power_ref, partial_ref, turned_ref, right_side_ref, *, near, batch,
):
    dates = left_ref.shape[0]
    band = halo_band()
    for t in range(dates):
        halo = edges(left_ref[t], right_ref[t])
        halo_ref[t] = halo
        turned_ref[t] = turn(halo)
        right_side_ref[t] = jnp.zeros((ROWS, LANES), F32)
    halos = [halo_ref[t] * halo_ref[t] for t in range(dates)]
    for t, parts in enumerate(windows(sums_ref, 2 * K * near, halos, band)):
        for g in range(GROUPS):
            power_ref[t, 8 * g : 8 * g + 8, :] = parts[g]

    def power(t, g):
        return power_ref[t, 8 * g : 8 * g + 8, :]

    def add(t, g, x):
        rows = pl.ds(8 * g, 8)
        right_side_ref[t, rows, :] = right_side_ref[t, rows, :] + x

    for begin in range(0, near, batch):
        group = range(begin, begin + batch)
        halos = halo_pairs(table_ref, lambda t: halo_ref[t], lambda t: turned_ref[t], group)
        looked = windows(sums_ref, 2 * K * begin, halos, band)
        for i, t in enumerate(group):
            finish(looked[2 * K * i : 2 * K * (i + 1)], t, table_ref, power, None, out_ref, add)
    for t in range(near):
        for g in range(GROUPS):
            out_ref[pl.ds(8 * g * FIELDS + K * dates + t, 8, stride=FIELDS), :] = right_side_ref[
                t, 8 * g : 8 * g + 8, :
            ]
    partial_ref[...] = right_side_ref[near:]


def far_kernel(
    table_ref, message_ref, near_halo_ref, corner_ref, near_power_ref, partial_ref, sums_ref,
    out_ref, right_side_ref, *, near,
):
    del message_ref
    dates = near_halo_ref.shape[0]
    total_dates = dates * lax.axis_size("date")
    first = lax.axis_index("date") * dates
    halo = {t: near_halo_ref[t] for t in range(near, dates)}
    for t in range(SPAN):
        halo[dates + t] = corner_ref[t]
        right_side_ref[t] = partial_ref[t]
        right_side_ref[SPAN + t] = jnp.zeros((ROWS, LANES), F32)
    turned = {t: turn(halo[t]) for t in halo}
    halos = [halo[t] * halo[t] for t in range(dates, dates + SPAN)]
    halos += halo_pairs(table_ref, lambda t: halo[t], lambda t: turned[t], range(near, dates))
    sums = windows(sums_ref, 0, halos, halo_band())

    def power(t, g):
        return sums[t - dates][g] if t >= dates else near_power_ref[t, 8 * g : 8 * g + 8, :]

    def add(t, g, x):
        rows = pl.ds(8 * g, 8)
        right_side_ref[t - near, rows, :] = right_side_ref[t - near, rows, :] + x

    for t in range(near, dates):
        n = SPAN + 2 * K * (t - near)
        limit = (total_dates - first - t).astype(F32)
        finish(sums[n : n + 2 * K], t, table_ref, power, limit, out_ref, add)
    for g in range(GROUPS):
        base = 8 * g * FIELDS + K * dates
        for t in range(near, dates + SPAN - 1):
            out_ref[pl.ds(base + t, 8, stride=FIELDS), :] = right_side_ref[
                t - near, 8 * g : 8 * g + 8, :
            ]
        out_ref[pl.ds(base + dates + SPAN - 1, 8, stride=FIELDS), :] = table_ref[K * dates]


def solve_kernel(
    recv_ref, coh_out, disp_ref, coh_ref, weight_ref, p_ref, r_ref, x_ref, q_ref, sem, *, dates
):
    quarters = recv_ref.shape[0] // (8 * FIELDS)
    chunk = 2 * FIELDS
    sub = rows_of((8, LANES))
    zero = jnp.zeros((8, LANES), F32)

    def received(quarter, f):
        return recv_ref[pl.ds(quarter * 8 * FIELDS + f, 8, stride=FIELDS), :]

    for d in range(4 * quarters):
        for row in range(2):
            coh_ref[pl.ds(d * 2 * K * dates + row, K * dates, stride=2), :] = recv_ref[
                pl.ds(d * chunk + row * FIELDS, K * dates), :
            ]
    copy = pltpu.make_async_copy(coh_ref, coh_out, sem)
    copy.start()

    def one_block_later(get, quarter):
        near = pltpu.roll(get(quarter), 6, 0)
        far = pltpu.roll(get(quarter + 1), 6, 0) if quarter + 1 < quarters else zero
        return jnp.where(sub < 6, near, far)

    def one_block_earlier(get, quarter):
        near = pltpu.roll(get(quarter), 2, 0)
        far = pltpu.roll(get(quarter - 1), 2, 0) if quarter > 0 else zero
        return jnp.where(sub >= 2, near, far)

    def over_dates(v):
        v = v + pltpu.roll(v, 4, 0)
        return v + pltpu.roll(v, 2, 0)

    def refresh_ghosts():
        for quarter in range(quarters):
            for e in range(SPAN):
                p_ref[quarter, SPAN + dates + e] = one_block_later(
                    lambda n: p_ref[n, SPAN + e], quarter
                )
                p_ref[quarter, e] = one_block_earlier(lambda n: p_ref[n, dates + e], quarter)

    rr = zero
    rims = []
    for quarter in range(quarters):
        rim = [received(quarter, K * dates + dates + e) for e in range(SPAN - 1)]
        rest = rim[0] + rim[1] + rim[2]
        for u in range(dates):
            rest = rest + received(quarter, K * dates + u)
        rims.append(rim + [-rest])
    for quarter in range(quarters):
        offsets = received(quarter, K * dates + dates + SPAN - 1)
        for u in range(dates):
            values = [received(quarter, K * u + k) for k in range(K)]
            places = [
                jnp.broadcast_to(offsets[:, K * u + k : K * u + k + 1], (8, LANES)) for k in range(K)
            ]
            for s in range(1, SPAN + 1):
                weight = zero
                for k in range(K):
                    weight = jnp.where(places[k] == float(s), values[k], weight)
                weight_ref[s - 1, quarter, SPAN + u] = weight
            b = received(quarter, K * dates + u)
            if u < SPAN:
                b = b + one_block_earlier(lambda n: rims[n][u], quarter)
            p_ref[quarter, SPAN + u] = b
            r_ref[quarter, u] = b
            x_ref[pl.ds((quarter * dates + u) * 8, 8), :] = zero
            rr = rr + b * b
    for quarter in range(quarters):
        for s in range(1, SPAN + 1):
            for e in range(SPAN - s, SPAN):
                weight_ref[s - 1, quarter, e] = one_block_earlier(
                    lambda n: weight_ref[s - 1, n, dates + e], quarter
                )
    rr = over_dates(rr)
    refresh_ghosts()

    def iteration(step, rr):
        pq = zero
        for quarter in range(quarters):
            flows = {}
            for e in range(dates + SPAN):
                here = p_ref[quarter, e]
                out = None
                for s in range(1, SPAN + 1):
                    if e >= SPAN - s:
                        flow = weight_ref[s - 1, quarter, e] * (p_ref[quarter, e + s] - here)
                        flows[s, e] = flow
                        if e >= SPAN:
                            term = flows.pop((s, e - s)) - flow
                            out = term if out is None else out + term
                if e >= SPAN:
                    out = out + DAMPING * here
                    q_ref[quarter, e - SPAN] = out
                    pq = pq + here * out
        a = rr / (over_dates(pq) + EPSILON)
        nn = zero
        for quarter in range(quarters):
            for u in range(dates):
                rows = pl.ds((quarter * dates + u) * 8, 8)
                x_ref[rows, :] = x_ref[rows, :] + a * p_ref[quarter, SPAN + u]
                rest = r_ref[quarter, u] - a * q_ref[quarter, u]
                r_ref[quarter, u] = rest
                nn = nn + rest * rest
        nn = over_dates(nn)
        ratio = nn / (rr + EPSILON)
        for quarter in range(quarters):
            for u in range(dates):
                p_ref[quarter, SPAN + u] = r_ref[quarter, u] + ratio * p_ref[quarter, SPAN + u]
        refresh_ghosts()
        return nn

    lax.fori_loop(0, ITERS, iteration, rr)
    for quarter in range(quarters):
        for j in range(4):
            for row in range(2):
                disp_ref[pl.ds((quarter * 4 + j) * 2 * dates + row, dates, stride=2), :] = x_ref[
                    pl.ds(quarter * dates * 8 + 2 * j + row, dates, stride=8), :
                ]
    copy.wait()


def vmem(count):
    return [pl.BlockSpec(memory_space=pltpu.VMEM)] * count


PARAMS = pltpu.CompilerParams(vmem_limit_bytes=48 * 1024 * 1024)


def shape(*sizes):
    return jax.ShapeDtypeStruct(sizes, F32)


def local(acquisitions, offsets):
    dates = acquisitions.shape[1]
    blocks = lax.axis_size("date")
    tiles = lax.axis_size("pix")
    near = dates - SPAN
    anywhere = [pl.BlockSpec(memory_space=pl.ANY)]
    offsets = offsets.T
    packed, kept, rim = pl.pallas_call(
        pack_kernel,
        out_shape=[
            shape(dates, 8, LANES), shape(2, dates, ROWS, LANES), shape(2, SPAN, ROWS, LANES),
        ],
        in_specs=vmem(1),
        out_specs=vmem(3),
        compiler_params=PARAMS,
    )(acquisitions)

    def moved(x, dates_back, tiles_on):
        route = [
            (p * blocks + d, (p + tiles_on) % tiles * blocks + (d - dates_back) % blocks)
            for p in range(tiles)
            for d in range(blocks)
        ]
        return lax.ppermute(x, ("pix", "date"), route)

    rim = moved(rim, 1, 0)
    left = moved(packed, 0, 1)
    right = moved(packed, 0, -1)

    sums, table = pl.pallas_call(
        functools.partial(center_kernel, near=near, batch=7),
        out_shape=[shape(2 * K * near + dates, ROWS, LANES), shape(K * dates + 1, 8, LANES)],
        in_specs=vmem(2),
        out_specs=vmem(2),
        compiler_params=PARAMS,
    )(offsets, kept)

    def corner_kernel(left_ref, right_ref, sums_ref, out_ref):
        del sums_ref
        for t in range(SPAN):
            out_ref[t] = edges(left_ref[t], right_ref[t])

    corner = pl.pallas_call(
        corner_kernel,
        out_shape=shape(SPAN, 8, LANES),
        in_specs=vmem(2) + anywhere,
        out_specs=vmem(1)[0],
        compiler_params=PARAMS,
    )(left, right, sums)
    corner = moved(corner, 1, 0)

    messages, halo, power, partial = pl.pallas_call(
        functools.partial(near_kernel, near=near, batch=7),
        out_shape=[
            shape(blocks * 2 * FIELDS, LANES),
            shape(dates, 8, LANES),
            shape(dates, ROWS, LANES),
            shape(SPAN, ROWS, LANES),
        ],
        in_specs=vmem(4),
        out_specs=vmem(4),
        scratch_shapes=[
            pltpu.VMEM((dates, 8, LANES), F32),
            pltpu.VMEM((dates, ROWS, LANES), F32),
        ],
        compiler_params=PARAMS,
    )(table, left, right, sums)

    far_sums = pl.pallas_call(
        functools.partial(far_center_kernel, near=near),
        out_shape=shape(SPAN + 2 * K * SPAN, ROWS, LANES),
        in_specs=vmem(3),
        out_specs=vmem(1)[0],
        compiler_params=PARAMS,
    )(table, kept, rim)

    messages = pl.pallas_call(
        functools.partial(far_kernel, near=near),
        out_shape=shape(blocks * 2 * FIELDS, LANES),
        in_specs=vmem(7),
        out_specs=vmem(1)[0],
        input_output_aliases={1: 0},
        scratch_shapes=[pltpu.VMEM((2 * SPAN, ROWS, LANES), F32)],
        compiler_params=PARAMS,
    )(table, messages, halo, corner, power, partial, far_sums)
    received = lax.all_to_all(messages, "date", split_axis=0, concat_axis=0, tiled=True)

    quarters = blocks // 4
    coherence, displacement = pl.pallas_call(
        functools.partial(solve_kernel, dates=dates),
        out_shape=[
            jax.ShapeDtypeStruct((blocks * dates * K * 2, LANES), F32),
            jax.ShapeDtypeStruct((blocks * dates * 2, LANES), F32),
        ],
        in_specs=vmem(1),
        out_specs=anywhere + vmem(1),
        scratch_shapes=[
            pltpu.VMEM((blocks * dates * K * 2, LANES), F32),
            pltpu.VMEM((SPAN, quarters, SPAN + dates, 8, LANES), F32),
            pltpu.VMEM((quarters, dates + 2 * SPAN, 8, LANES), F32),
            pltpu.VMEM((quarters, dates, 8, LANES), F32),
            pltpu.VMEM((quarters * dates * 8, LANES), F32),
            pltpu.VMEM((quarters, dates, 8, LANES), F32),
            pltpu.SemaphoreType.DMA,
        ],
        compiler_params=PARAMS,
    )(received)
    return (
        coherence.reshape(blocks * dates, K, 2, LANES),
        displacement.reshape(blocks * dates, 2, LANES),
    )


def solution(mesh):
    placed = (P(None, "date", None, "pix"), P("date", None))
    return jax.shard_map(
        local,
        mesh=mesh,
        in_specs=placed,
        out_specs=(P(None, None, "date", "pix"), P(None, "date", "pix")),
        check_vma=False,
    )
```

time: 46.5 us -> 43.4 us (0.933)
  Pallas kernels: 9.75 us -> 6.74 us
  waiting for transfers between devices: 0.01 us -> 2.84 us
  blocking collectives: 26.1 us -> 23.9 us
  starting transfers between devices: 7.91 us -> 6.68 us
    ppermute x4, waiting for transfers between devices: 0.01 us -> 2.84 us  [moved(): return lax.ppermute(x, ('pix', 'date'), route)]
    all_to_all x1, blocking collectives: 26.1 us -> 23.9 us  [local(): lax.all_to_all(messages, 'date', split_axis=0, concat_axis=0, tiled=True)]
    pallas_call x1, Pallas kernels: 3.04 us -> 1.16 us  [local(): pl.pallas_call(functools.partial(near_kernel, near=near, batch=7), out_sh...]
    ppermute x4, starting transfers between devices: 7.91 us -> 6.68 us  [moved(): return lax.ppermute(x, ('pix', 'date'), route)]
    pallas_call x1, Pallas kernels: 1.36 us -> 0.44 us  [local(): pl.pallas_call(functools.partial(far_kernel, near=near), out_shape=shape(...]
  transfers between devices with their start and end apart: 4 -> 4, of which waited for: 0 -> 2; matrix products, arithmetic and copies ran while one was open for 0% -> 0% of each run, Pallas kernels for 10% -> 6%
where the time goes in v2:
time: 43.4 us; the launch traced here: 42.6 us
  blocking collectives  23.9 us (55%)
  Pallas kernels  6.74 us (16%)
  starting transfers between devices  6.68 us (15%)
  waiting for transfers between devices  2.84 us (7%)
  local copies, waits for them, and re-layouts  1.74 us (4%)
  between operations  0.7 us (2%)
    all_to_all x1, blocking collectives, local(): lax.all_to_all(messages, 'date', split_axis=0, concat_axis=0, tiled=True)  23.9 us
    ppermute x4, starting transfers between devices, moved(): return lax.ppermute(x, ('pix', 'date'), route)  6.68 us
    pallas_call x1, Pallas kernels, local(): pl.pallas_call(functools.partial(solve_kernel, dates=dates), out_shape=[j...  3.45 us
    ppermute x4, waiting for transfers between devices, moved(): return lax.ppermute(x, ('pix', 'date'), route)  2.84 us
    unnamed x4, local copies, waits for them, and re-layouts  1.74 us
    pallas_call x1, Pallas kernels, local(): pl.pallas_call(functools.partial(near_kernel, near=near, batch=7), out_sh...  1.16 us
    pallas_call x1, Pallas kernels, local(): pl.pallas_call(functools.partial(center_kernel, near=near, batch=7), out_...  1.13 us
  transfers between devices with their start and end apart: 4, of which 2 were waited for; matrix products, arithmetic and copies ran while one was open for 0% of the time, Pallas kernels for 6%

profile of v2, /device:TPU:32, one launch (start us, length us, event | category | flops | bytes accessed | tf_op | source)
XLA Modules:
  0.0 42.6 jit_solution(11226886450013195588)
XLA Ops:
  0.6 0.0 copy-start
  0.6 1.1 %copy-done = f32[2,18,32,128]{3,2,1,0:T(8,128)S(1)} copy-done((f32[2,18,32,128]{3,2,1,0:T(8,128)S(1)}, f32[2,18,32,128]{3,2,1,0:T(8,128)}, u32[]{:S(2)}) %copy-start) | copy-done | bytes 589848
  1.7 0.2 shard_map.41
  1.9 5.3 %collective-permute-start.3 = (f32[2,4,32,128]{3,2,1,0:T(8,128)S(1)}, f32[2,4,32,128]{3,2,1,0:T(8,128)S(1)}, u32[]{:S(2)}, u32[]{:S(2)}) collective-permute-start(f32[2,4,32,128]{3,2,1,0:T(8,128)S(1)} %get-tuple-element.21), channel_id=1, source_target_pairs={{0,15},{1,0},{2,1},{3,2},{4,3},{5,4},{6,5},{7,6},{8,7},{9,8},{10,9... | collective-permute-start | bytes 393224 | tf_op jit(solution)/shard_map/ppermute | solution.py:485
  7.2 0.0 collective-permute-start.1
  7.2 0.5 %collective-permute-start = (f32[18,8,128]{2,1,0:T(8,128)S(1)}, f32[18,8,128]{2,1,0:T(8,128)S(1)}, u32[]{:S(2)}, u32[]{:S(2)}) collective-permute-start(f32[18,8,128]{2,1,0:T(8,128)S(1)} %get-tuple-element.15), channel_id=1, source_target_pairs={{0,16},{1,17},{2,18},{3,19},{4,20},{5,21},{6,22},{7,23},{8,24},{9,... | collective-permute-start | bytes 221192 | tf_op jit(solution)/shard_map/ppermute | solution.py:485
  7.7 0.0 copy-start.1
  7.7 0.7 %copy-done.1 = s32[18,3]{0,1:T(4,128)S(1)} copy-done((s32[18,3]{0,1:T(4,128)S(1)}, s32[18,3]{0,1:T(4,128)}, u32[]{:S(2)}) %copy-start.1) | copy-done | bytes 240
  8.4 1.1 %shard_map.42 = (f32[102,32,128]{2,1,0:T(8,128)S(1)}, f32[55,8,128]{2,1,0:T(8,128)S(1)}) custom-call(s32[3,18]{1,0:T(4,128)S(1)} %bitcast.7, f32[2,18,32,128]{3,2,1,0:T(8,128)S(1)} %get-tuple-element.13.acq_ref), custom_call_target="tpu_custom_call" | custom-call | tf_op jit(solution)/shard_map/pallas_call | solution.py:491
  9.5 0.0 collective-permute-done.1.right_ref
  9.5 1.4 %collective-permute-done.left_ref = f32[18,8,128]{2,1,0:T(8,128)S(1)} collective-permute-done((f32[18,8,128]{2,1,0:T(8,128)S(1)}, f32[18,8,128]{2,1,0:T(8,128)S(1)}, u32[]{:S(2)}, u32[]{:S(2)}) %collective-permute-start) | collective-permute-done | bytes 73760 | tf_op jit(solution)/shard_map/ppermute | solution.py:485
  11.0 0.9 %collective-permute-start.2 = (f32[4,8,128]{2,1,0:T(8,128)S(1)}, f32[4,8,128]{2,1,0:T(8,128)S(1)}, u32[]{:S(2)}, u32[]{:S(2)}) collective-permute-start(f32[4,8,128]{2,1,0:T(8,128)S(1)} %shard_map.44), channel_id=1, source_target_pairs={{0,15},{1,0},{2,1},{3,2},{4,3},{5,4},{6,5},{7,6},{8,7},{9,8},{10,9... | collective-permute-start | bytes 49160 | tf_op jit(solution)/shard_map/ppermute | solution.py:485
  11.9 1.2 %shard_map.43 = (f32[2432,128]{1,0:T(8,128)S(1)}, f32[18,8,128]{2,1,0:T(8,128)S(1)}, f32[18,32,128]{2,1,0:T(8,128)S(1)}, f32[4,32,128]{2,1,0:T(8,128)S(1)}) custom-call(f32[55,8,128]{2,1,0:T(8,128)S(1)} %get-tuple-element.14.table_ref, f32[18,8,128]{2,1,0:T(8,128)S(1)} %collective-permute-done.left_ref, f32[18,8,128]{2,1,0:T(8,128)S(1)} %collective-permute-done.1.right_ref, ...), custom_call_target="tpu_custom_call" | custom-call | tf_op jit(solution)/shard_map/pallas_call | solution.py:513
  13.1 0.0 collective-permute-done.3.rim_ref
  13.1 0.3 shard_map.45.sums_ref
  13.4 1.4 %collective-permute-done.2.corner_ref = f32[4,8,128]{2,1,0:T(8,128)S(1)} collective-permute-done((f32[4,8,128]{2,1,0:T(8,128)S(1)}, f32[4,8,128]{2,1,0:T(8,128)S(1)}, u32[]{:S(2)}, u32[]{:S(2)}) %collective-permute-start.2) | collective-permute-done | bytes 16416 | tf_op jit(solution)/shard_map/ppermute | solution.py:485
  14.8 0.4 %shard_map.46 = f32[2432,128]{1,0:T(8,128)S(1)} custom-call(f32[55,8,128]{2,1,0:T(8,128)S(1)} %get-tuple-element.14.table_ref, f32[2432,128]{1,0:T(8,128)S(1)} %get-tuple-element.17.message_ref, f32[18,8,128]{2,1,0:T(8,128)S(1)} %get-tuple-element.18.near_halo_ref, ...), custom_call_target="tpu_custom_call", output_to_operand_aliasing={{}: (1, {})} | custom-call | tf_op jit(solution)/shard_map/pallas_call | solution.py:538
  15.3 23.9 %all_to_all.11 = f32[16,152,128]{2,1,0:T(8,128)S(1)} all-to-all(f32[16,152,128]{2,1,0:T(8,128)S(1)} %bitcast.5), channel_id=1, replica_groups=mesh['pix'=8,'date'=16] {'date'}, dimensions={0} | all-to-all | bytes 2490368 | tf_op jit(solution)/shard_map/all_to_all | solution.py:547
  39.2 3.4 %shard_map.47 = (f32[1728,128]{1,0:T(8,128)}, f32[576,128]{1,0:T(8,128)}) custom-call(f32[2432,128]{1,0:T(8,128)S(1)} %bitcast.6), custom_call_target="tpu_custom_call" | custom-call | tf_op jit(solution)/shard_map/pallas_call | solution.py:550
  (1 shorter events, 0.0 us)
Async XLA Ops:
  0.6 1.1 %copy-start = (f32[2,18,32,128]{3,2,1,0:T(8,128)S(1)}, f32[2,18,32,128]{3,2,1,0:T(8,128)}, u32[]{:S(2)}) copy-start(f32[2,18,32,128]{3,2,1,0:T(8,128)} %acq_ref.1) | copy-start | bytes 1769476
  1.9 11.1 %collective-permute-start.3 = (f32[2,4,32,128]{3,2,1,0:T(8,128)S(1)}, f32[2,4,32,128]{3,2,1,0:T(8,128)S(1)}, u32[]{:S(2)}, u32[]{:S(2)}) collective-permute-start(f32[2,4,32,128]{3,2,1,0:T(8,128)S(1)} %get-tuple-element.21), channel_id=1, source_target_pairs={{0,15},{1,0},{2,1},{3,2},{4,3},{5,4},{6,5},{7,6},{8,7},{9,8},{10,9... | collective-permute-start | bytes 393224 | tf_op jit(solution)/shard_map/ppermute | solution.py:485
  7.2 2.3 %collective-permute-start.1 = (f32[18,8,128]{2,1,0:T(8,128)S(1)}, f32[18,8,128]{2,1,0:T(8,128)S(1)}, u32[]{:S(2)}, u32[]{:S(2)}) collective-permute-start(f32[18,8,128]{2,1,0:T(8,128)S(1)} %get-tuple-element.15), channel_id=1, source_target_pairs={{0,112},{1,113},{2,114},{3,115},{4,116},{5,117},{6,118},{7,119},{8... | collective-permute-start | bytes 221192 | tf_op jit(solution)/shard_map/ppermute | solution.py:485
  7.2 3.8 %collective-permute-start = (f32[18,8,128]{2,1,0:T(8,128)S(1)}, f32[18,8,128]{2,1,0:T(8,128)S(1)}, u32[]{:S(2)}, u32[]{:S(2)}) collective-permute-start(f32[18,8,128]{2,1,0:T(8,128)S(1)} %get-tuple-element.15), channel_id=1, source_target_pairs={{0,16},{1,17},{2,18},{3,19},{4,20},{5,21},{6,22},{7,23},{8,24},{9,... | collective-permute-start | bytes 221192 | tf_op jit(solution)/shard_map/ppermute | solution.py:485
  7.7 0.7 %copy-start.1 = (s32[18,3]{0,1:T(4,128)S(1)}, s32[18,3]{0,1:T(4,128)}, u32[]{:S(2)}) copy-start(s32[18,3]{0,1:T(4,128)} %param.3) | copy-start | bytes 652
  11.0 3.8 %collective-permute-start.2 = (f32[4,8,128]{2,1,0:T(8,128)S(1)}, f32[4,8,128]{2,1,0:T(8,128)S(1)}, u32[]{:S(2)}, u32[]{:S(2)}) collective-permute-start(f32[4,8,128]{2,1,0:T(8,128)S(1)} %shard_map.44), channel_id=1, source_target_pairs={{0,15},{1,0},{2,1},{3,2},{4,3},{5,4},{6,5},{7,6},{8,7},{9,8},{10,9... | collective-permute-start | bytes 49160 | tf_op jit(solution)/shard_map/ppermute | solution.py:485

commit v3 on v2

--- a/solution.py
+++ b/solution.py
@@ -47,12 +47,12 @@
         packed_ref[t] = total
 
 
-def edges(left, right):
+def edges(twin, other):
     tile, tiles = lax.axis_index("pix"), lax.axis_size("pix")
-    lane = lanes_of(left.shape) % 16
+    lane = lanes_of(twin.shape) % 16
     low = jnp.where(tile == 0, HC, 0)
     high = jnp.where(tile == tiles - 1, HC, 2 * HC)
-    both = jnp.where(lane < HC, left, right)
+    both = jnp.where((lane < HC) == (tile % 2 == 1), twin, other)
     return jnp.where((lane >= low) & (lane < high), both, 0.0)
 
 
@@ -327,7 +327,8 @@
 
 
 def solve_kernel(
-    recv_ref, coh_out, disp_ref, coh_ref, weight_ref, p_ref, r_ref, x_ref, q_ref, sem, *, dates
+    recv_ref, coh_out, disp_out,
+    coh_ref, disp_ref, weight_ref, p_ref, r_ref, x_ref, q_ref, sems, *, dates,
 ):
     quarters = recv_ref.shape[0] // (8 * FIELDS)
     chunk = 2 * FIELDS
@@ -342,7 +343,7 @@
             coh_ref[pl.ds(d * 2 * K * dates + row, K * dates, stride=2), :] = recv_ref[
                 pl.ds(d * chunk + row * FIELDS, K * dates), :
             ]
-    copy = pltpu.make_async_copy(coh_ref, coh_out, sem)
+    copy = pltpu.make_async_copy(coh_ref, coh_out, sems.at[0])
     copy.start()
 
     def one_block_later(get, quarter):
@@ -403,7 +404,7 @@
     rr = over_dates(rr)
     refresh_ghosts()
 
-    def iteration(step, rr):
+    def step_size(rr):
         pq = zero
         for quarter in range(quarters):
             flows = {}
@@ -421,7 +422,10 @@
                     out = out + DAMPING * here
                     q_ref[quarter, e - SPAN] = out
                     pq = pq + here * out
-        a = rr / (over_dates(pq) + EPSILON)
+        return rr / (over_dates(pq) + EPSILON)
+
+    def iteration(step, rr):
+        a = step_size(rr)
         nn = zero
         for quarter in range(quarters):
             for u in range(dates):
@@ -438,14 +442,24 @@
         refresh_ghosts()
         return nn
 
-    lax.fori_loop(0, ITERS, iteration, rr)
+    a = step_size(lax.fori_loop(0, ITERS - 1, iteration, rr))
+    copies = [copy]
     for quarter in range(quarters):
+        for u in range(dates):
+            rows = pl.ds((quarter * dates + u) * 8, 8)
+            x_ref[rows, :] = x_ref[rows, :] + a * p_ref[quarter, SPAN + u]
         for j in range(4):
             for row in range(2):
                 disp_ref[pl.ds((quarter * 4 + j) * 2 * dates + row, dates, stride=2), :] = x_ref[
                     pl.ds(quarter * dates * 8 + 2 * j + row, dates, stride=8), :
                 ]
-    copy.wait()
+        span = pl.ds(quarter * 8 * dates, 8 * dates)
+        copies.append(
+            pltpu.make_async_copy(disp_ref.at[span], disp_out.at[span], sems.at[1 + quarter])
+        )
+        copies[-1].start()
+    for copy in copies:
+        copy.wait()
 
 
 def vmem(count):
@@ -476,17 +490,29 @@
         compiler_params=PARAMS,
     )(acquisitions)
 
-    def moved(x, dates_back, tiles_on):
-        route = [
-            (p * blocks + d, (p + tiles_on) % tiles * blocks + (d - dates_back) % blocks)
-            for p in range(tiles)
-            for d in range(blocks)
-        ]
+    def moved(x, partner, dates_back):
+        route = []
+        for p in range(tiles):
+            for d in range(blocks):
+                source = (d + dates_back) % blocks
+                if partner(p) is None:
+                    route.append((p * blocks + (source if dates_back else d ^ 1), p * blocks + d))
+                else:
+                    route.append((partner(p) * blocks + source, p * blocks + d))
         return lax.ppermute(x, ("pix", "date"), route)
 
-    rim = moved(rim, 1, 0)
-    left = moved(packed, 0, 1)
-    right = moved(packed, 0, -1)
+    def same(p):
+        return p
+
+    def twin(p):
+        return p ^ 1
+
+    def other(p):
+        return None if p in (0, tiles - 1) else p + 1 if p % 2 else p - 1
+
+    rim = moved(rim, same, 1)
+    left = moved(packed, twin, 0)
+    right = moved(packed, other, 0)
 
     sums, table = pl.pallas_call(
         functools.partial(center_kernel, near=near, batch=7),
@@ -508,7 +534,7 @@
         out_specs=vmem(1)[0],
         compiler_params=PARAMS,
     )(left, right, sums)
-    corner = moved(corner, 1, 0)
+    corner = moved(corner, same, 1)
 
     messages, halo, power, partial = pl.pallas_call(
         functools.partial(near_kernel, near=near, batch=7),
@@ -554,15 +580,16 @@
             jax.ShapeDtypeStruct((blocks * dates * 2, LANES), F32),
         ],
         in_specs=vmem(1),
-        out_specs=anywhere + vmem(1),
+        out_specs=anywhere * 2,
         scratch_shapes=[
             pltpu.VMEM((blocks * dates * K * 2, LANES), F32),
+            pltpu.VMEM((blocks * dates * 2, LANES), F32),
             pltpu.VMEM((SPAN, quarters, SPAN + dates, 8, LANES), F32),
             pltpu.VMEM((quarters, dates + 2 * SPAN, 8, LANES), F32),
             pltpu.VMEM((quarters, dates, 8, LANES), F32),
             pltpu.VMEM((quarters * dates * 8, LANES), F32),
             pltpu.VMEM((quarters, dates, 8, LANES), F32),
-            pltpu.SemaphoreType.DMA,
+            pltpu.SemaphoreType.DMA((1 + quarters,)),
         ],
         compiler_params=PARAMS,
     )(received)

time: 43.4 us -> 43 us (level)
  starting transfers between devices: 6.68 us -> 8.21 us
  waiting for transfers between devices: 2.84 us -> 1.41 us
    ppermute x4, starting transfers between devices: 6.68 us -> 8.21 us  [moved(): return lax.ppermute(x, ('pix', 'date'), route)]
    ppermute x4, waiting for transfers between devices: 2.84 us -> 1.41 us  [moved(): return lax.ppermute(x, ('pix', 'date'), route)]
  transfers between devices with their start and end apart: 4 -> 4, of which waited for: 2 -> 1; matrix products, arithmetic and copies ran while one was open for 0% -> 0% of each run, Pallas kernels for 6% -> 6%
where the time goes in v3:
time: 43 us; the launch traced here: 42.4 us
  blocking collectives  23.9 us (56%)
  starting transfers between devices  8.21 us (19%)
  Pallas kernels  6.51 us (15%)
  local copies, waits for them, and re-layouts  1.74 us (4%)
  waiting for transfers between devices  1.41 us (3%)
  between operations  0.71 us (2%)
    all_to_all x1, blocking collectives, local(): lax.all_to_all(messages, 'date', split_axis=0, concat_axis=0, tiled=True)  23.9 us
    ppermute x4, starting transfers between devices, moved(): return lax.ppermute(x, ('pix', 'date'), route)  8.21 us
    pallas_call x1, Pallas kernels, local(): pl.pallas_call(functools.partial(solve_kernel, dates=dates), out_shape=[j...  3.21 us
    unnamed x4, local copies, waits for them, and re-layouts  1.74 us
    ppermute x4, waiting for transfers between devices, moved(): return lax.ppermute(x, ('pix', 'date'), route)  1.41 us
    pallas_call x1, Pallas kernels, local(): pl.pallas_call(functools.partial(near_kernel, near=near, batch=7), out_sh...  1.15 us
    pallas_call x1, Pallas kernels, local(): pl.pallas_call(functools.partial(center_kernel, near=near, batch=7), out_...  1.13 us
  transfers between devices with their start and end apart: 4, of which 1 were waited for; matrix products, arithmetic and copies ran while one was open for 0% of the time, Pallas kernels for 6%

profile of v3, /device:TPU:32, one launch (start us, length us, event | category | flops | bytes accessed | tf_op | source)
XLA Modules:
  0.0 42.4 jit_solution(9349468788754032370)
XLA Ops:
  0.6 0.0 copy-start
  0.6 1.1 %copy-done = f32[2,18,32,128]{3,2,1,0:T(8,128)S(1)} copy-done((f32[2,18,32,128]{3,2,1,0:T(8,128)S(1)}, f32[2,18,32,128]{3,2,1,0:T(8,128)}, u32[]{:S(2)}) %copy-start) | copy-done | bytes 589848
  1.7 0.2 shard_map.41
  1.9 5.3 %collective-permute-start.3 = (f32[2,4,32,128]{3,2,1,0:T(8,128)S(1)}, f32[2,4,32,128]{3,2,1,0:T(8,128)S(1)}, u32[]{:S(2)}, u32[]{:S(2)}) collective-permute-start(f32[2,4,32,128]{3,2,1,0:T(8,128)S(1)} %get-tuple-element.21), channel_id=1, source_target_pairs={{1,0},{2,1},{3,2},{4,3},{5,4},{6,5},{7,6},{8,7},{9,8},{10,9},{11,1... | collective-permute-start | bytes 393224 | tf_op jit(solution)/shard_map/ppermute | solution.py:502
  7.2 0.0 collective-permute-start.1
  7.2 2.0 %collective-permute-start = (f32[18,8,128]{2,1,0:T(8,128)S(1)}, f32[18,8,128]{2,1,0:T(8,128)S(1)}, u32[]{:S(2)}, u32[]{:S(2)}) collective-permute-start(f32[18,8,128]{2,1,0:T(8,128)S(1)} %get-tuple-element.15), channel_id=1, source_target_pairs={{16,0},{17,1},{18,2},{19,3},{20,4},{21,5},{22,6},{23,7},{24,8},{25... | collective-permute-start | bytes 221192 | tf_op jit(solution)/shard_map/ppermute | solution.py:502
  9.2 0.0 copy-start.1
  9.2 0.7 %copy-done.1 = s32[18,3]{0,1:T(4,128)S(1)} copy-done((s32[18,3]{0,1:T(4,128)S(1)}, s32[18,3]{0,1:T(4,128)}, u32[]{:S(2)}) %copy-start.1) | copy-done | bytes 240
  9.9 1.1 %shard_map.42 = (f32[102,32,128]{2,1,0:T(8,128)S(1)}, f32[55,8,128]{2,1,0:T(8,128)S(1)}) custom-call(s32[3,18]{1,0:T(4,128)S(1)} %bitcast.7, f32[2,18,32,128]{3,2,1,0:T(8,128)S(1)} %get-tuple-element.13.acq_ref), custom_call_target="tpu_custom_call" | custom-call | tf_op jit(solution)/shard_map/pallas_call | solution.py:517
  11.1 0.0 collective-permute-done.1.right_ref
  11.1 0.0 collective-permute-done.left_ref
  11.1 0.9 %collective-permute-start.2 = (f32[4,8,128]{2,1,0:T(8,128)S(1)}, f32[4,8,128]{2,1,0:T(8,128)S(1)}, u32[]{:S(2)}, u32[]{:S(2)}) collective-permute-start(f32[4,8,128]{2,1,0:T(8,128)S(1)} %shard_map.44), channel_id=1, source_target_pairs={{1,0},{2,1},{3,2},{4,3},{5,4},{6,5},{7,6},{8,7},{9,8},{10,9},{11,1... | collective-permute-start | bytes 49160 | tf_op jit(solution)/shard_map/ppermute | solution.py:502
  12.0 1.2 %shard_map.43 = (f32[2432,128]{1,0:T(8,128)S(1)}, f32[18,8,128]{2,1,0:T(8,128)S(1)}, f32[18,32,128]{2,1,0:T(8,128)S(1)}, f32[4,32,128]{2,1,0:T(8,128)S(1)}) custom-call(f32[55,8,128]{2,1,0:T(8,128)S(1)} %get-tuple-element.14.table_ref, f32[18,8,128]{2,1,0:T(8,128)S(1)} %collective-permute-done.left_ref, f32[18,8,128]{2,1,0:T(8,128)S(1)} %collective-permute-done.1.right_ref, ...), custom_call_target="tpu_custom_call" | custom-call | tf_op jit(solution)/shard_map/pallas_call | solution.py:539
  13.2 0.0 collective-permute-done.3.rim_ref
  13.2 0.3 shard_map.45.sums_ref
  13.5 1.4 %collective-permute-done.2.corner_ref = f32[4,8,128]{2,1,0:T(8,128)S(1)} collective-permute-done((f32[4,8,128]{2,1,0:T(8,128)S(1)}, f32[4,8,128]{2,1,0:T(8,128)S(1)}, u32[]{:S(2)}, u32[]{:S(2)}) %collective-permute-start.2) | collective-permute-done | bytes 16416 | tf_op jit(solution)/shard_map/ppermute | solution.py:502
  14.9 0.4 %shard_map.46 = f32[2432,128]{1,0:T(8,128)S(1)} custom-call(f32[55,8,128]{2,1,0:T(8,128)S(1)} %get-tuple-element.14.table_ref, f32[2432,128]{1,0:T(8,128)S(1)} %get-tuple-element.17.message_ref, f32[18,8,128]{2,1,0:T(8,128)S(1)} %get-tuple-element.18.near_halo_ref, ...), custom_call_target="tpu_custom_call", output_to_operand_aliasing={{}: (1, {})} | custom-call | tf_op jit(solution)/shard_map/pallas_call | solution.py:564
  15.4 23.9 %all_to_all.11 = f32[16,152,128]{2,1,0:T(8,128)S(1)} all-to-all(f32[16,152,128]{2,1,0:T(8,128)S(1)} %bitcast.5), channel_id=1, replica_groups=mesh['pix'=8,'date'=16] {'date'}, dimensions={0} | all-to-all | bytes 2490368 | tf_op jit(solution)/shard_map/all_to_all | solution.py:573
  39.2 3.2 %shard_map.47 = (f32[1728,128]{1,0:T(8,128)}, f32[576,128]{1,0:T(8,128)}) custom-call(f32[2432,128]{1,0:T(8,128)S(1)} %bitcast.6), custom_call_target="tpu_custom_call" | custom-call | tf_op jit(solution)/shard_map/pallas_call | solution.py:576
  (1 shorter events, 0.0 us)
Async XLA Ops:
  0.6 1.1 %copy-start = (f32[2,18,32,128]{3,2,1,0:T(8,128)S(1)}, f32[2,18,32,128]{3,2,1,0:T(8,128)}, u32[]{:S(2)}) copy-start(f32[2,18,32,128]{3,2,1,0:T(8,128)} %acq_ref.1) | copy-start | bytes 1769476
  1.9 11.2 %collective-permute-start.3 = (f32[2,4,32,128]{3,2,1,0:T(8,128)S(1)}, f32[2,4,32,128]{3,2,1,0:T(8,128)S(1)}, u32[]{:S(2)}, u32[]{:S(2)}) collective-permute-start(f32[2,4,32,128]{3,2,1,0:T(8,128)S(1)} %get-tuple-element.21), channel_id=1, source_target_pairs={{1,0},{2,1},{3,2},{4,3},{5,4},{6,5},{7,6},{8,7},{9,8},{10,9},{11,1... | collective-permute-start | bytes 393224 | tf_op jit(solution)/shard_map/ppermute | solution.py:502
  7.2 3.9 %collective-permute-start.1 = (f32[18,8,128]{2,1,0:T(8,128)S(1)}, f32[18,8,128]{2,1,0:T(8,128)S(1)}, u32[]{:S(2)}, u32[]{:S(2)}) collective-permute-start(f32[18,8,128]{2,1,0:T(8,128)S(1)} %get-tuple-element.15), channel_id=1, source_target_pairs={{1,0},{0,1},{3,2},{2,3},{5,4},{4,5},{7,6},{6,7},{9,8},{8,9},{11,10... | collective-permute-start | bytes 221192 | tf_op jit(solution)/shard_map/ppermute | solution.py:502
  7.2 3.9 %collective-permute-start = (f32[18,8,128]{2,1,0:T(8,128)S(1)}, f32[18,8,128]{2,1,0:T(8,128)S(1)}, u32[]{:S(2)}, u32[]{:S(2)}) collective-permute-start(f32[18,8,128]{2,1,0:T(8,128)S(1)} %get-tuple-element.15), channel_id=1, source_target_pairs={{16,0},{17,1},{18,2},{19,3},{20,4},{21,5},{22,6},{23,7},{24,8},{25... | collective-permute-start | bytes 221192 | tf_op jit(solution)/shard_map/ppermute | solution.py:502
  9.2 0.7 %copy-start.1 = (s32[18,3]{0,1:T(4,128)S(1)}, s32[18,3]{0,1:T(4,128)}, u32[]{:S(2)}) copy-start(s32[18,3]{0,1:T(4,128)} %param.3) | copy-start | bytes 652
  11.1 3.8 %collective-permute-start.2 = (f32[4,8,128]{2,1,0:T(8,128)S(1)}, f32[4,8,128]{2,1,0:T(8,128)S(1)}, u32[]{:S(2)}, u32[]{:S(2)}) collective-permute-start(f32[4,8,128]{2,1,0:T(8,128)S(1)} %shard_map.44), channel_id=1, source_target_pairs={{1,0},{2,1},{3,2},{4,3},{5,4},{6,5},{7,6},{8,7},{9,8},{10,9},{11,1... | collective-permute-start | bytes 49160 | tf_op jit(solution)/shard_map/ppermute | solution.py:502

commit v4 on v3

--- a/solution.py
+++ b/solution.py
@@ -520,6 +520,7 @@
         in_specs=vmem(2),
         out_specs=vmem(2),
         compiler_params=PARAMS,
+        cost_estimate=pl.CostEstimate(flops=20000000000, transcendentals=0, bytes_accessed=60000000),
     )(offsets, kept)
 
     def corner_kernel(left_ref, right_ref, sums_ref, out_ref):
@@ -533,6 +534,7 @@
         in_specs=vmem(2) + anywhere,
         out_specs=vmem(1)[0],
         compiler_params=PARAMS,
+        cost_estimate=pl.CostEstimate(flops=10000000, transcendentals=0, bytes_accessed=30000),
     )(left, right, sums)
     corner = moved(corner, same, 1)
 
@@ -551,6 +553,7 @@
             pltpu.VMEM((dates, ROWS, LANES), F32),
         ],
         compiler_params=PARAMS,
+        cost_estimate=pl.CostEstimate(flops=20000000000, transcendentals=0, bytes_accessed=60000000),
     )(table, left, right, sums)
 
     far_sums = pl.pallas_call(
@@ -559,6 +562,7 @@
         in_specs=vmem(3),
         out_specs=vmem(1)[0],
         compiler_params=PARAMS,
+        cost_estimate=pl.CostEstimate(flops=1000000000, transcendentals=0, bytes_accessed=3000000),
     )(table, kept, rim)
 
     messages = pl.pallas_call(
@@ -569,6 +573,7 @@
         input_output_aliases={1: 0},
         scratch_shapes=[pltpu.VMEM((2 * SPAN, ROWS, LANES), F32)],
         compiler_params=PARAMS,
+        cost_estimate=pl.CostEstimate(flops=1000000000, transcendentals=0, bytes_accessed=3000000),
     )(table, messages, halo, corner, power, partial, far_sums)
     received = lax.all_to_all(messages, "date", split_axis=0, concat_axis=0, tiled=True)
 
@@ -592,6 +597,7 @@
             pltpu.SemaphoreType.DMA((1 + quarters,)),
         ],
         compiler_params=PARAMS,
+        cost_estimate=pl.CostEstimate(flops=1000000000, transcendentals=0, bytes_accessed=3000000),
     )(received)
     return (
         coherence.reshape(blocks * dates, K, 2, LANES),

time: 43 us -> 42.8 us (level)
  no operation moved by 1% of the time
where the time goes in v4:
time: 42.8 us; the launch traced here: 42.5 us
  blocking collectives  23.9 us (56%)
  starting transfers between devices  8.21 us (19%)
  Pallas kernels  6.52 us (15%)
  local copies, waits for them, and re-layouts  1.74 us (4%)
  waiting for transfers between devices  1.4 us (3%)
  between operations  0.72 us (2%)
    all_to_all x1, blocking collectives, local(): lax.all_to_all(messages, 'date', split_axis=0, concat_axis=0, tiled=True)  23.9 us
    ppermute x4, starting transfers between devices, moved(): return lax.ppermute(x, ('pix', 'date'), route)  8.21 us
    pallas_call x1, Pallas kernels, local(): pl.pallas_call(functools.partial(solve_kernel, dates=dates), out_shape=[j...  3.21 us
    unnamed x4, local copies, waits for them, and re-layouts  1.74 us
    ppermute x4, waiting for transfers between devices, moved(): return lax.ppermute(x, ('pix', 'date'), route)  1.4 us
    pallas_call x1, Pallas kernels, local(): pl.pallas_call(functools.partial(near_kernel, near=near, batch=7), out_sh...  1.15 us
    pallas_call x1, Pallas kernels, local(): pl.pallas_call(functools.partial(center_kernel, near=near, batch=7), out_...  1.13 us
  transfers between devices with their start and end apart: 4, of which 1 were waited for; matrix products, arithmetic and copies ran while one was open for 0% of the time, Pallas kernels for 6%

profile of v4, /device:TPU:32, one launch (start us, length us, event | category | flops | bytes accessed | tf_op | source)
XLA Modules:
  0.0 42.5 jit_solution(2334497764290079289)
XLA Ops:
  0.6 0.0 copy-start
  0.6 1.1 %copy-done = f32[2,18,32,128]{3,2,1,0:T(8,128)S(1)} copy-done((f32[2,18,32,128]{3,2,1,0:T(8,128)S(1)}, f32[2,18,32,128]{3,2,1,0:T(8,128)}, u32[]{:S(2)}) %copy-start) | copy-done | bytes 589848
  1.7 0.2 shard_map.41
  1.9 0.1 collective-permute-start.1
  2.0 2.0 %collective-permute-start = (f32[18,8,128]{2,1,0:T(8,128)S(1)}, f32[18,8,128]{2,1,0:T(8,128)S(1)}, u32[]{:S(2)}, u32[]{:S(2)}) collective-permute-start(f32[18,8,128]{2,1,0:T(8,128)S(1)} %get-tuple-element.15), channel_id=1, source_target_pairs={{16,0},{17,1},{18,2},{19,3},{20,4},{21,5},{22,6},{23,7},{24,8},{25... | collective-permute-start | bytes 221192 | tf_op jit(solution)/shard_map/ppermute | solution.py:502
  4.0 5.2 %collective-permute-start.3 = (f32[2,4,32,128]{3,2,1,0:T(8,128)S(1)}, f32[2,4,32,128]{3,2,1,0:T(8,128)S(1)}, u32[]{:S(2)}, u32[]{:S(2)}) collective-permute-start(f32[2,4,32,128]{3,2,1,0:T(8,128)S(1)} %get-tuple-element.21), channel_id=1, source_target_pairs={{1,0},{2,1},{3,2},{4,3},{5,4},{6,5},{7,6},{8,7},{9,8},{10,9},{11,1... | collective-permute-start | bytes 393224 | tf_op jit(solution)/shard_map/ppermute | solution.py:502
  9.2 0.0 copy-start.1
  9.3 0.7 %copy-done.1 = s32[18,3]{0,1:T(4,128)S(1)} copy-done((s32[18,3]{0,1:T(4,128)S(1)}, s32[18,3]{0,1:T(4,128)}, u32[]{:S(2)}) %copy-start.1) | copy-done | bytes 240
  9.9 1.1 %shard_map.42 = (f32[102,32,128]{2,1,0:T(8,128)S(1)}, f32[55,8,128]{2,1,0:T(8,128)S(1)}) custom-call(s32[3,18]{1,0:T(4,128)S(1)} %bitcast.7, f32[2,18,32,128]{3,2,1,0:T(8,128)S(1)} %get-tuple-element.13.acq_ref), custom_call_target="tpu_custom_call" | custom-call | flops 20000000000 | bytes 60000000 | tf_op jit(solution)/shard_map/pallas_call | solution.py:517
  11.1 0.0 collective-permute-done.1.right_ref
  11.1 0.0 collective-permute-done.left_ref
  11.1 0.9 %collective-permute-start.2 = (f32[4,8,128]{2,1,0:T(8,128)S(1)}, f32[4,8,128]{2,1,0:T(8,128)S(1)}, u32[]{:S(2)}, u32[]{:S(2)}) collective-permute-start(f32[4,8,128]{2,1,0:T(8,128)S(1)} %shard_map.44), channel_id=1, source_target_pairs={{1,0},{2,1},{3,2},{4,3},{5,4},{6,5},{7,6},{8,7},{9,8},{10,9},{11,1... | collective-permute-start | bytes 49160 | tf_op jit(solution)/shard_map/ppermute | solution.py:502
  12.0 1.2 %shard_map.43 = (f32[2432,128]{1,0:T(8,128)S(1)}, f32[18,8,128]{2,1,0:T(8,128)S(1)}, f32[18,32,128]{2,1,0:T(8,128)S(1)}, f32[4,32,128]{2,1,0:T(8,128)S(1)}) custom-call(f32[55,8,128]{2,1,0:T(8,128)S(1)} %get-tuple-element.14.table_ref, f32[18,8,128]{2,1,0:T(8,128)S(1)} %collective-permute-done.left_ref, f32[18,8,128]{2,1,0:T(8,128)S(1)} %collective-permute-done.1.right_ref, ...), custom_call_target="tpu_custom_call" | custom-call | flops 20000000000 | bytes 60000000 | tf_op jit(solution)/shard_map/pallas_call | solution.py:541
  13.2 0.0 collective-permute-done.3.rim_ref
  13.2 0.3 shard_map.45.sums_ref
  13.5 1.4 %collective-permute-done.2.corner_ref = f32[4,8,128]{2,1,0:T(8,128)S(1)} collective-permute-done((f32[4,8,128]{2,1,0:T(8,128)S(1)}, f32[4,8,128]{2,1,0:T(8,128)S(1)}, u32[]{:S(2)}, u32[]{:S(2)}) %collective-permute-start.2) | collective-permute-done | bytes 16416 | tf_op jit(solution)/shard_map/ppermute | solution.py:502
  14.9 0.4 %shard_map.46 = f32[2432,128]{1,0:T(8,128)S(1)} custom-call(f32[55,8,128]{2,1,0:T(8,128)S(1)} %get-tuple-element.14.table_ref, f32[2432,128]{1,0:T(8,128)S(1)} %get-tuple-element.17.message_ref, f32[18,8,128]{2,1,0:T(8,128)S(1)} %get-tuple-element.18.near_halo_ref, ...), custom_call_target="tpu_custom_call", output_to_operand_aliasing={{}: (1, {})} | custom-call | flops 1000000000 | bytes 3000000 | tf_op jit(solution)/shard_map/pallas_call | solution.py:568
  15.4 23.9 %all_to_all.11 = f32[16,152,128]{2,1,0:T(8,128)S(1)} all-to-all(f32[16,152,128]{2,1,0:T(8,128)S(1)} %bitcast.5), channel_id=1, replica_groups=mesh['pix'=8,'date'=16] {'date'}, dimensions={0} | all-to-all | bytes 2490368 | tf_op jit(solution)/shard_map/all_to_all | solution.py:578
  39.3 3.2 %shard_map.47 = (f32[1728,128]{1,0:T(8,128)}, f32[576,128]{1,0:T(8,128)}) custom-call(f32[2432,128]{1,0:T(8,128)S(1)} %bitcast.6), custom_call_target="tpu_custom_call" | custom-call | flops 1000000000 | bytes 3000000 | tf_op jit(solution)/shard_map/pallas_call | solution.py:581
  (1 shorter events, 0.0 us)
Async XLA Ops:
  0.6 1.1 %copy-start = (f32[2,18,32,128]{3,2,1,0:T(8,128)S(1)}, f32[2,18,32,128]{3,2,1,0:T(8,128)}, u32[]{:S(2)}) copy-start(f32[2,18,32,128]{3,2,1,0:T(8,128)} %acq_ref.1) | copy-start | bytes 1769476
  1.9 9.1 %collective-permute-start.1 = (f32[18,8,128]{2,1,0:T(8,128)S(1)}, f32[18,8,128]{2,1,0:T(8,128)S(1)}, u32[]{:S(2)}, u32[]{:S(2)}) collective-permute-start(f32[18,8,128]{2,1,0:T(8,128)S(1)} %get-tuple-element.15), channel_id=1, source_target_pairs={{1,0},{0,1},{3,2},{2,3},{5,4},{4,5},{7,6},{6,7},{9,8},{8,9},{11,10... | collective-permute-start | bytes 221192 | tf_op jit(solution)/shard_map/ppermute | solution.py:502
  2.0 9.1 %collective-permute-start = (f32[18,8,128]{2,1,0:T(8,128)S(1)}, f32[18,8,128]{2,1,0:T(8,128)S(1)}, u32[]{:S(2)}, u32[]{:S(2)}) collective-permute-start(f32[18,8,128]{2,1,0:T(8,128)S(1)} %get-tuple-element.15), channel_id=1, source_target_pairs={{16,0},{17,1},{18,2},{19,3},{20,4},{21,5},{22,6},{23,7},{24,8},{25... | collective-permute-start | bytes 221192 | tf_op jit(solution)/shard_map/ppermute | solution.py:502
  4.0 9.1 %collective-permute-start.3 = (f32[2,4,32,128]{3,2,1,0:T(8,128)S(1)}, f32[2,4,32,128]{3,2,1,0:T(8,128)S(1)}, u32[]{:S(2)}, u32[]{:S(2)}) collective-permute-start(f32[2,4,32,128]{3,2,1,0:T(8,128)S(1)} %get-tuple-element.21), channel_id=1, source_target_pairs={{1,0},{2,1},{3,2},{4,3},{5,4},{6,5},{7,6},{8,7},{9,8},{10,9},{11,1... | collective-permute-start | bytes 393224 | tf_op jit(solution)/shard_map/ppermute | solution.py:502
  9.2 0.7 %copy-start.1 = (s32[18,3]{0,1:T(4,128)S(1)}, s32[18,3]{0,1:T(4,128)}, u32[]{:S(2)}) copy-start(s32[18,3]{0,1:T(4,128)} %param.3) | copy-start | bytes 652
  11.1 3.8 %collective-permute-start.2 = (f32[4,8,128]{2,1,0:T(8,128)S(1)}, f32[4,8,128]{2,1,0:T(8,128)S(1)}, u32[]{:S(2)}, u32[]{:S(2)}) collective-permute-start(f32[4,8,128]{2,1,0:T(8,128)S(1)} %shard_map.44), channel_id=1, source_target_pairs={{1,0},{2,1},{3,2},{4,3},{5,4},{6,5},{7,6},{8,7},{9,8},{10,9},{11,1... | collective-permute-start | bytes 49160 | tf_op jit(solution)/shard_map/ppermute | solution.py:502
